TPU v7x, 256 devices: a whole 4x4x8 slice. The times are simulated.
256 devices in a mesh: batch: 4 (over x), tm: 16 (over z, core), label: 4 (over y).
Axes of the slice: x: 4, y: 4, z: 8, core: 2. Of those that a mesh axis runs over, the one named last changes fastest.
Arguments:
- enc_joint: bfloat16 [4, 384, 640], P('batch', 'tm'), may hold values from -6 to 6
- pred_joint: bfloat16 [4, 320, 640], P('batch', 'label'), may hold values from -6 to 6
- out_weight: bfloat16 [640, 4096], P('batch', 'tm'), may hold values from -1.1953125 to 1.1953125
- labels: int32 [4, 320], P('batch', 'label'), may hold values from 0 to 4095
- frame_len: int32 [4], P('batch'), may hold values from 192 to 384, as said below
- label_len: int32 [4], P('batch'), may hold values from 80 to 319, as said below
Outputs:
- log_blank: float32 [4, 384, 320], P('batch', 'tm', 'label')
- log_label: float32 [4, 384, 320], P('batch', 'tm', 'label')
- loss: float32 [4], P('batch')
Inputs may be any that keep to these rules, and one draw needn't show every extreme that they name: `frame_len`: some utterance has 384 frames. `label_len`: some utterance has 319 labels.
All inputs are finite; a program needn't handle non-finite values.
Results may differ from a plain program's by a relative error of at most 0.00063.
Values may be sent and summed in bfloat16 or wider, within the bound.
No kernel may reach another device: no remote copies, remote signals or barrier semaphores. Data moves between devices by JAX's collectives and lax.ppermute only.
A program may use at most 128 MiB of HBM per device.

v0:
```python
import functools

import jax
import jax.numpy as jnp
from jax import lax
from jax.experimental import pallas as pl
from jax.experimental.pallas import tpu as pltpu
from jax.sharding import PartitionSpec as P

NEG = -1e30
F32 = jnp.float32
BF16 = jnp.bfloat16
SPAN = 8
GROUP = 4
CHUNKS = 2
LABEL_WAYS = 4
BATCH_WAYS = 4


def pack_kernel(place_ref, weight_ref, pred_ref, labels_ref, block_ref, packed_ref):
    mine, odd_block = place_ref[0], lax.rem(place_ref[3], 2) == 1
    tiles, positions, _ = packed_ref.shape
    rows = block_ref.shape[0]
    lane = lax.broadcasted_iota(jnp.int32, (rows, 128), 1)
    values = jnp.where(mine < 2, weight_ref[:, :128].astype(F32), weight_ref[:, 128:].astype(F32))
    left = jnp.where(odd_block, values[rows:], values[:rows])
    right = jnp.where(odd_block, values[:rows], values[rows:])
    second = lax.rem(mine, 2) == 1
    left = jnp.where(second, pltpu.roll(left, 64, 1), left)
    right = jnp.where(second, right, pltpu.roll(right, 64, 1))
    block_ref[...] = jnp.where(lane < 64, left, right).astype(BF16)
    for tile in range(tiles - 1):
        packed_ref[tile] = pred_ref[:, 128 * tile:128 * tile + 128]
    labels = jnp.broadcast_to(labels_ref[...], (positions, positions))
    across = lax.broadcasted_iota(jnp.int32, (positions, positions), 0)
    along = lax.broadcasted_iota(jnp.int32, (positions, positions), 1)
    own = jnp.where(across == along, labels, 0)
    high = jnp.sum((own >> 6).astype(F32), axis=1, keepdims=True)
    low = jnp.sum((own & 63).astype(F32), axis=1, keepdims=True)
    lane = lax.broadcasted_iota(jnp.int32, (positions, 128), 1)
    packed_ref[tiles - 1] = jnp.where(lane == 0, high, jnp.where(lane == 1, low, 0.0)).astype(BF16)


def pack(place, weight, pred, labels):
    positions, width = pred.shape
    vmem = pl.BlockSpec(memory_space=pltpu.VMEM)
    return pl.pallas_call(
        pack_kernel,
        out_shape=(
            jax.ShapeDtypeStruct((weight.shape[0] // 2, 128), BF16),
            jax.ShapeDtypeStruct((width // 128 + 1, positions, 128), BF16),
        ),
        in_specs=[pl.BlockSpec(memory_space=pltpu.SMEM)] + [vmem] * 3,
        out_specs=(vmem, vmem),
        name="pack",
    )(place, weight, pred, labels)


def joint_kernel(
    place_ref, enc_ref, own_ref, own_pred_ref, mine_ref, theirs_ref,
    lse_ref, blank_ref, picked_ref,
    enc, pred, chosen, picks, columns_first, weight, hidden_a, hidden_b, logits_a, logits_b, top, total, top_a, top_b,
):
    mine, batch, core = place_ref[0], place_ref[1], place_ref[2]
    frames, width = enc_ref.shape
    tiles, positions, _ = pred.shape
    share = weight.shape[0]
    chunk = share // CHUNKS
    enc[...] = enc_ref[...].astype(F32)
    blocks, half_rows, _ = own_ref.shape
    some = blocks // 2
    lane = lax.broadcasted_iota(jnp.int32, (half_rows, 128), 1)

    def put_rows(ref, start, count, source, first_pair):
        at = pl.multiple_of(source * 2 * half_rows, 8)
        for pair in range(count // 2):
            left = ref[start + 2 * pair].astype(F32)
            right = ref[start + 2 * pair + 1].astype(F32)
            columns_first[first_pair + pair, pl.ds(at, half_rows), :] = jnp.where(lane < 64, left, right)
            columns_first[first_pair + pair, pl.ds(at + half_rows, half_rows), :] = jnp.where(lane < 64, right, left)

    def put_positions(ref, start, count, source, first):
        at = pl.multiple_of(source * half_rows, 8)
        for index in range(count):
            pred[first + index, pl.ds(at, half_rows), :] = ref[start + index].astype(F32)

    def wrap(value, ways):
        return lax.rem(value + ways, ways)

    put_rows(own_ref, 0, blocks, batch, 0)
    put_positions(own_pred_ref, 0, tiles, mine, 0)
    for ref, side in ((mine_ref, core), (theirs_ref, 1 - core)):
        step = 2 * side - 1
        put_rows(ref, 0, blocks, wrap(batch + step, BATCH_WAYS), 0)
        put_rows(ref, blocks, some, wrap(batch + 2, BATCH_WAYS), side * (some // 2))
        put_positions(ref, blocks + some, tiles, wrap(mine + step, LABEL_WAYS), 0)
        put_positions(ref, blocks + some + tiles, tiles // 2, wrap(mine + 2, LABEL_WAYS), side * (tiles // 2))
    depth = lax.broadcasted_iota(jnp.int32, (128, width), 1)
    upper = lax.rem(depth, 2 * half_rows) < half_rows
    for tile in range(share // 128):
        turned = columns_first[tile].T
        swapped = jnp.concatenate([turned[64:], turned[:64]], axis=0)
        weight[128 * tile:128 * tile + 128, :] = jnp.where(upper, turned, swapped).astype(BF16)

    digits = pred[tiles - 1]
    high = digits[:, 0:1].astype(jnp.int32)
    low = digits[:, 1:2].astype(jnp.int32)
    spot = jnp.where((high & 3) == mine, (high >> 2) * 64 + low, -1)
    columns = lax.broadcasted_iota(jnp.int32, (positions, share), 1)
    one_hot = (columns == spot).astype(F32).astype(BF16)
    chosen[...] = jnp.dot(one_hot, weight[...], preferred_element_type=F32)
    picks[...] = jnp.zeros_like(picks)
    lanes = lax.broadcasted_iota(jnp.int32, picks.shape, 1)

    def make_hidden(frame, part, out):
        rows = slice(part * positions, (part + 1) * positions)
        picked = jnp.zeros((positions, 128), F32)
        frame_row = enc[pl.ds(frame, 1), :]
        for tile in range(tiles - 1):
            strip = slice(128 * tile, 128 * tile + 128)
            rounded = jnp.tanh(pred[tile] + frame_row[:, strip]).astype(BF16)
            out[rows, strip] = rounded
            picked = picked + rounded.astype(F32) * chosen[:, strip]
        picked = jnp.sum(picked, axis=1, keepdims=True)
        picks[...] = jnp.where(lanes == frame, picked, picks[...])

    def multiply(part, hidden, out, chunk_top):
        acc = lax.dot_general(
            weight[part * chunk:(part + 1) * chunk, :], hidden[...],
            (((1,), (1,)), ((), ())), preferred_element_type=F32,
        )
        out[...] = acc
        chunk_top[...] = jnp.max(acc, axis=0, keepdims=True)

    def gather_terms(part, group, logits, chunk_top):
        values = logits[...]
        high = chunk_top[...]
        if part == 0:
            blank_ref[pl.ds(group, 1), :] = logits[0:1, :]
            total[...] = jnp.sum(jnp.exp(values - high), axis=0, keepdims=True)
            top[...] = high
        else:
            high = jnp.maximum(high, top[...])
            total[...] = total[...] * jnp.exp(top[...] - high) + jnp.sum(
                jnp.exp(values - high), axis=0, keepdims=True
            )
            top[...] = high
        if part == CHUNKS - 1:
            lse_ref[pl.ds(group, 1), :] = top[...] + jnp.log(total[...])

    groups = frames // GROUP
    for part in range(GROUP):
        make_hidden(part, part, hidden_a)
    logits_b[...] = jnp.zeros_like(logits_b)
    top[...] = jnp.zeros_like(top)
    top_b[...] = jnp.zeros_like(top)
    total[...] = jnp.ones_like(total)
    each = GROUP // CHUNKS

    def half(group, now, later):
        for part in range(CHUNKS):
            fresh, old = (logits_a, logits_b) if part % 2 == 0 else (logits_b, logits_a)
            fresh_top, old_top = (top_a, top_b) if part % 2 == 0 else (top_b, top_a)
            multiply(part, now, fresh, fresh_top)
            for which in range(part * each, (part + 1) * each):
                make_hidden(jnp.minimum(group + 1, groups - 1) * GROUP + which, which, later)
            if part == 0:
                gather_terms(CHUNKS - 1, jnp.maximum(group - 1, 0), old, old_top)
            else:
                gather_terms(part - 1, group, old, old_top)

    def step(pair, carry):
        half(2 * pair, hidden_a, hidden_b)
        half(2 * pair + 1, hidden_b, hidden_a)
        return carry

    lax.fori_loop(0, groups // 2, step, 0)
    gather_terms(CHUNKS - 1, groups - 1, logits_b, top_b)
    picked_ref[...] = picks[...].T[:frames, :]


def joint_terms(place, enc, own, own_pred, mine, theirs):
    frames, width = enc.shape
    tiles = own_pred.shape[0]
    positions = LABEL_WAYS * own_pred.shape[1]
    share = 64 * own.shape[0]
    wide = GROUP * positions
    grouped = jax.ShapeDtypeStruct((frames // GROUP, wide), F32)
    vmem = pl.BlockSpec(memory_space=pltpu.VMEM)
    smem = pl.BlockSpec(memory_space=pltpu.SMEM)
    flops = 2 * frames * positions * width * share
    return pl.pallas_call(
        joint_kernel,
        out_shape=(grouped, grouped, jax.ShapeDtypeStruct((frames, positions), F32)),
        in_specs=[smem] + [vmem] * 5,
        out_specs=(vmem,) * 3,
        scratch_shapes=[
            pltpu.VMEM((frames, width), F32),
            pltpu.VMEM((tiles, positions, 128), F32),
            pltpu.VMEM((positions, width), F32),
            pltpu.VMEM((positions, 128), F32),
            pltpu.VMEM((share // 128, width, 128), F32),
            pltpu.VMEM((share, width), BF16),
            pltpu.VMEM((wide, width), BF16),
            pltpu.VMEM((wide, width), BF16),
            pltpu.VMEM((share // CHUNKS, wide), F32),
            pltpu.VMEM((share // CHUNKS, wide), F32),
            pltpu.VMEM((1, wide), F32),
            pltpu.VMEM((1, wide), F32),
            pltpu.VMEM((1, wide), F32),
            pltpu.VMEM((1, wide), F32),
        ],
        compiler_params=pltpu.CompilerParams(vmem_limit_bytes=48 << 20),
        cost_estimate=pl.CostEstimate(flops=flops, bytes_accessed=2 << 20, transcendentals=0),
        name="joint",
    )(place, enc, own, own_pred, mine, theirs)


def tree(combine, terms):
    while len(terms) > 1:
        pairs = [combine(a, b) for a, b in zip(terms[::2], terms[1::2])]
        terms = pairs + terms[len(terms) - len(terms) % 2:]
    return terms[0]


def log_sum(terms):
    if len(terms) == 1:
        return terms[0]
    if len(terms) == 2:
        gap = jnp.minimum(*terms) - jnp.maximum(*terms)
        return jnp.maximum(*terms) + jnp.log(1.0 + jnp.exp(gap))
    top = tree(jnp.maximum, terms)
    return top + jnp.log(tree(jnp.add, [jnp.exp(term - top) for term in terms]))


def shift_lanes(values, by):
    by = by % values.shape[1]
    return values if by == 0 else pltpu.roll(values, by, 1)


def compose(first, then):
    terms = []
    for count in range(len(first) + len(then) - 1):
        parts = [
            then[late] + shift_lanes(first[count - late], late)
            for late in range(len(then))
            if 0 <= count - late < len(first)
        ]
        terms.append(log_sum(parts))
    return terms


def shear(values, lead):
    rows = values.shape[0]
    lanes = lax.broadcasted_iota(jnp.int32, values.shape, 1)
    if lead:
        values = pltpu.roll(values, rows - lead, 0)
    for bit in (64, 32, 16, 8, 4, 2, 1):
        values = jnp.where((lanes & bit) != 0, pltpu.roll(values, bit, 0), values)
    return values


def lattice_kernel(
    frame_len_ref, label_len_ref, grid_ref, loss_ref, stay, move, ahead, back, ahead_far, back_far
):
    blocks, _, frames_dev, positions = grid_ref.shape
    frames = blocks * frames_dev
    strips, diagonals, _ = stay.shape
    lanes_all = 128 * strips
    flen = frame_len_ref[0]
    ulen = label_len_ref[0]
    spare = jnp.full((frames, lanes_all - positions), NEG, F32)
    tall = frames + 128
    pad = jnp.full((tall - frames, 128), NEG, F32)

    def whole(which):
        rows = jnp.concatenate([grid_ref[block, which] for block in range(blocks)], axis=0)
        return jnp.concatenate([rows, spare], axis=1)

    blank = whole(0)
    label = shift_lanes(whole(1), 1)
    stay[...] = jnp.full(stay.shape, NEG, F32)
    move[...] = jnp.full(move.shape, NEG, F32)
    for part in range(strips):
        start = 128 * part
        rows = min(tall, diagonals - start)
        for source, out, lead in ((blank, stay, 0), (label, move, 1)):
            strip = jnp.concatenate([source[:, start:start + 128], pad], axis=0)
            out[part, start:start + rows, :] = shear(strip, lead)[:rows]

    depth = SPAN * SPAN
    for group in range(diagonals // depth):
        base = group * depth
        live = [p for p in range(strips) if 128 * p <= base + depth and base < 128 * p + 128 + frames]
        first, count_live = live[0], len(live)
        row = lax.broadcasted_iota(jnp.int32, (SPAN, 128 * count_live), 0)
        lane = lax.broadcasted_iota(jnp.int32, (SPAN, 128 * count_live), 1) + 128 * first
        in_row = lane < positions
        moves_in = in_row & (lane > 0)
        rest = jnp.where(lane == ulen, 0.0, NEG)
        steps = []
        for step in range(SPAN):
            time = base + row * SPAN + step - lane
            at = pl.ds(base + step, SPAN, stride=SPAN)
            held = jnp.concatenate([stay[part, at, :] for part in live], axis=1)
            moved = jnp.concatenate([move[part, at, :] for part in live], axis=1)
            held = jnp.where(in_row & (time < flen), held, rest)
            moved = jnp.where(moves_in & (time + 1 < flen), moved, NEG)
            steps.append([held, moved])
        while len(steps) > 1:
            steps = [compose(steps[i], steps[i + 1]) for i in range(0, len(steps), 2)]
        at = group * SPAN
        for count, values in enumerate(steps[0]):
            moved = shift_lanes(values, -count)
            for part in range(strips):
                if part in live:
                    strip = slice(128 * (part - first), 128 * (part - first) + 128)
                    forth, from_back = values[:, strip], moved[:, strip]
                else:
                    forth = jnp.full((SPAN, 128), NEG, F32)
                    if count == 0:
                        lane = lax.broadcasted_iota(jnp.int32, (SPAN, 128), 1) + 128 * part
                        forth = jnp.where(lane == ulen, 0.0, NEG)
                    from_back = forth
                if count < SPAN:
                    ahead[part, pl.ds(at * SPAN + count, SPAN, stride=SPAN), :] = forth
                    back[part, pl.ds(at * SPAN + SPAN - 1 - count, SPAN, stride=SPAN), :] = from_back
                else:
                    ahead_far[at:at + SPAN, 128 * part:128 * part + 128] = forth
                    back_far[at:at + SPAN, 128 * part:128 * part + 128] = from_back

    spans = diagonals // SPAN
    place = lax.broadcasted_iota(jnp.int32, (1, lanes_all), 1)

    def advance(state, shift, table, far, block, far_shift):
        rows = pl.ds(pl.multiple_of(block * SPAN, SPAN), SPAN)
        weights = jnp.concatenate([table[part, rows, :] for part in range(strips)], axis=1)
        spread = jnp.broadcast_to(state, (SPAN, lanes_all))
        near = weights + pltpu.roll(spread, shift, 1, stride=1, stride_axis=0)
        last = far[pl.ds(block, 1), :] + shift_lanes(state, far_shift)
        top = jnp.maximum(jnp.max(near, axis=0, keepdims=True), last)
        total = jnp.sum(jnp.exp(near - top), axis=0, keepdims=True) + jnp.exp(last - top)
        return top + jnp.log(total)

    def sweep(index, carry):
        alpha, beta = carry
        alpha = advance(alpha, 0, ahead, ahead_far, index, SPAN)
        beta = advance(beta, lanes_all - SPAN + 1, back, back_far, spans - 1 - index, -SPAN)
        return alpha, beta

    alpha = jnp.where(place == 0, 0.0, NEG)
    beta = jnp.where(place == ulen, 0.0, NEG)
    alpha, beta = lax.fori_loop(0, spans // 2, sweep, (alpha, beta))
    both = alpha + beta
    top = jnp.max(both, axis=1, keepdims=True)
    value = top + jnp.log(jnp.sum(jnp.exp(both - top), axis=1, keepdims=True))
    loss_ref[...] = -value / jnp.full((1, 1), flen, jnp.int32).astype(F32)


def lattice_loss(frame_len, label_len, grid):
    blocks, _, frames_dev, positions = grid.shape
    lanes = -(-positions // 128) * 128
    diagonals = -(-(blocks * frames_dev + positions) // (SPAN * SPAN)) * SPAN * SPAN
    assert (diagonals // SPAN) % 2 == 0
    strip = pltpu.VMEM((lanes // 128, diagonals, 128), F32)
    table = pltpu.VMEM((lanes // 128, diagonals, 128), F32)
    far = pltpu.VMEM((diagonals // SPAN, lanes), F32)
    vmem = pl.BlockSpec(memory_space=pltpu.VMEM)
    smem = pl.BlockSpec(memory_space=pltpu.SMEM)
    return pl.pallas_call(
        lattice_kernel,
        out_shape=jax.ShapeDtypeStruct((1, 1), F32),
        in_specs=[smem, smem, vmem],
        out_specs=vmem,
        scratch_shapes=[
            strip,
            strip,
            table,
            table,
            far,
            far,
        ],
        compiler_params=pltpu.CompilerParams(vmem_limit_bytes=40 << 20),
        name="lattice",
    )(frame_len, label_len, grid)


def around(array, axis):
    size = lax.axis_size(axis)
    moved = [
        lax.ppermute(array, axis, [(i, (i + by) % size) for i in range(size)])
        for by in range(1, size)
    ]
    return [array] + moved


def both_ways(array, axis):
    ways, cores = lax.axis_size(axis), lax.axis_size("tm")
    axes = ("batch", "tm") if axis == "batch" else ("tm", "label")

    def device(way, at):
        return way % ways * cores + at if axis == "batch" else at * ways + way % ways

    near, opposite = [], []
    for way in range(ways):
        for at in range(cores):
            near.append((device(way, at), device(way + (1 if at % 2 == 0 else -1), at)))
            opposite.append((device(way, at), device(way + 2, at)))
    some = array.shape[0] // 2
    half = lax.dynamic_slice_in_dim(array, lax.axis_index("tm") % 2 * some, some, axis=0)
    return lax.ppermute(array, axes, near), lax.ppermute(half, axes, opposite)


def shards(enc_joint, pred_joint, out_weight, labels, frame_len, label_len):
    positions = pred_joint.shape[1]
    mine = lax.axis_index("label")
    here = lax.axis_index("tm")
    place = jnp.stack([mine, lax.axis_index("batch"), here % 2, here]).astype(jnp.int32)
    own, own_pred = pack(place, out_weight, pred_joint[0], labels)
    with jax.named_scope("gather_weight"):
        own = lax.all_gather(own, "tm", axis=0, tiled=False)
    with jax.named_scope("fetch"):
        from_others = jnp.concatenate([*both_ways(own, "batch"), *both_ways(own_pred, "label")], axis=0)
        swap = [(i, i ^ 1) for i in range(lax.axis_size("tm"))]
        theirs = lax.ppermute(from_others, "tm", swap)
    lse, blank, picked = joint_terms(place, enc_joint[0], own, own_pred, from_others, theirs)
    with jax.named_scope("combine_vocab"):
        blank = jnp.where(mine == 0, blank, 0.0)
        parts = jnp.stack([lse.reshape(picked.shape), blank.reshape(picked.shape), picked])
        parts = around(parts, "label")
        top = functools.reduce(jnp.maximum, [part[0] for part in parts])
        norm = top + jnp.log(sum(jnp.exp(part[0] - top) for part in parts))
        log_blank = sum(part[1] for part in parts) - norm
        log_label = sum(part[2] for part in parts) - norm
    out_blank = lax.dynamic_slice_in_dim(log_blank, mine * positions, positions, axis=1)
    out_label = lax.dynamic_slice_in_dim(log_label, mine * positions, positions, axis=1)
    with jax.named_scope("gather_grid"):
        grid = lax.all_gather(jnp.stack([log_blank, log_label]), "tm", axis=0, tiled=False)
    loss = lattice_loss(frame_len, label_len, grid).reshape(1)
    return out_blank[None], out_label[None], loss


def solution(mesh):
    return jax.shard_map(
        shards,
        mesh=mesh,
        in_specs=(
            P("batch", "tm", None),
            P("batch", "label", None),
            P("batch", "tm"),
            P("batch", "label"),
            P("batch"),
            P("batch"),
        ),
        out_specs=(P("batch", "tm", "label"), P("batch", "tm", "label"), P("batch")),
        check_vma=False,
    )
```

profile of v0, /device:TPU:1, one launch (start us, length us, event | category | flops | bytes accessed | tf_op | source)
XLA Modules:
  0.0 100.3 jit_solution(1545370070739588561)
XLA Ops:
  0.6 0.6 pad_add_fusion.place_ref
  1.2 0.0 copy-start.1
  1.2 0.0 copy-start.2
  1.2 1.7 %pack.1 = (bf16[80,128]{1,0:T(8,128)(2,1)}, bf16[6,80,128]{2,1,0:T(8,128)(2,1)}) custom-call(s32[4]{0:T(128)} %pad_add_fusion.place_ref, bf16[160,256]{1,0:T(8,128)(2,1)} %weight_ref.1, bf16[80,640]{1,0:T(8,128)(2,1)} %bitcast.106, s32[1,80]{1,0:T(1,128)} %labels_ref.1), custom_call_target="tpu_custom_call" | custom-call | tf_op jit(solution)/shard_map/pack/pallas_call | solution.py:47
  3.0 0.0 copy-start
  3.0 22.6 %all-gather = bf16[1280,128]{1,0:T(8,128)(2,1)S(1)} all-gather(bf16[80,128]{1,0:T(8,128)(2,1)} %get-tuple-element.8), channel_id=2, replica_groups=mesh['batch'=4,'tm'=16,'label'=4] {'tm'}, dimensions={0}, use_global_device_ids=true | all-gather | bytes 348160 | tf_op jit(solution)/shard_map/gather_weight/all_gather | solution.py:421
  25.6 2.5 %collective-permute-start = (bf16[16,80,128]{2,1,0:T(8,128)(2,1)S(1)}, bf16[16,80,128]{2,1,0:T(8,128)(2,1)S(1)}, u32[]{:S(2)}, u32[]{:S(2)}) collective-permute-start(bf16[16,80,128]{2,1,0:T(8,128)(2,1)S(1)} %bitcast.100), channel_id=1, source_target_pairs={{0,64},{4,196},{8,72},{12,204},{16,80},{20,212},{24,88},{28,220},{... | collective-permute-start | bytes 983048 | tf_op jit(solution)/shard_map/fetch/ppermute | solution.py:411
  28.0 0.6 collective-permute-start.1
  28.7 2.7 %collective-permute-start.2 = (bf16[6,80,128]{2,1,0:T(8,128)(2,1)}, bf16[6,80,128]{2,1,0:T(8,128)(2,1)S(1)}, u32[]{:S(2)}, u32[]{:S(2)}) collective-permute-start(bf16[6,80,128]{2,1,0:T(8,128)(2,1)} %get-tuple-element.9.own_pred_ref), channel_id=1, source_target_pairs={{0,1},{4,7},{8,9},{12,15},{16,17},{20,23},{24,25},{28,31},{32,33},... | collective-permute-start | bytes 368648 | tf_op jit(solution)/shard_map/fetch/ppermute | solution.py:411
  31.4 0.9 constant_dynamic-slice_fusion
  32.3 0.3 collective-permute-start.3
  32.6 3.0 %collective-permute-done = bf16[16,80,128]{2,1,0:T(8,128)(2,1)S(1)} collective-permute-done((bf16[16,80,128]{2,1,0:T(8,128)(2,1)S(1)}, bf16[16,80,128]{2,1,0:T(8,128)(2,1)S(1)}, u32[]{:S(2)}, u32[]{:S(2)}) %collective-permute-start) | collective-permute-done | bytes 327712 | tf_op jit(solution)/shard_map/fetch/ppermute | solution.py:411
  35.6 0.0 collective-permute-done.1
  35.6 0.0 collective-permute-done.2
  35.7 2.1 %collective-permute-done.3 = bf16[3,80,128]{2,1,0:T(8,128)(2,1)S(1)} collective-permute-done((bf16[3,80,128]{2,1,0:T(8,128)(2,1)S(1)}, bf16[3,80,128]{2,1,0:T(8,128)(2,1)S(1)}, u32[]{:S(2)}, u32[]{:S(2)}) %collective-permute-start.3) | collective-permute-done | bytes 61472 | tf_op jit(solution)/shard_map/fetch/ppermute | solution.py:411
  37.7 1.3 %collective-permute-start.4 = (bf16[33,80,128]{2,1,0:T(8,128)(2,1)S(1)}, bf16[33,80,128]{2,1,0:T(8,128)(2,1)S(1)}, u32[]{:S(2)}, u32[]{:S(2)}) collective-permute-start(bf16[33,80,128]{2,1,0:T(8,128)(2,1)S(1)} %constant_dynamic-update-slice_fusion.mine_ref), channel_id=1, source_target_pairs={{0,4},{4,0},{8,12},{12,8},{16,20},{20,16},{24,28},{28,24},{32,36},... | collective-permute-start | bytes 2027528 | tf_op jit(solution)/shard_map/fetch/ppermute | solution.py:425
  39.0 1.8 %collective-permute-done.4.theirs_ref = bf16[33,80,128]{2,1,0:T(8,128)(2,1)S(1)} collective-permute-done((bf16[33,80,128]{2,1,0:T(8,128)(2,1)S(1)}, bf16[33,80,128]{2,1,0:T(8,128)(2,1)S(1)}, u32[]{:S(2)}, u32[]{:S(2)}) %collective-permute-start.4) | collective-permute-done | bytes 675872 | tf_op jit(solution)/shard_map/fetch/ppermute | solution.py:425
  40.8 0.0 copy-done.1
  40.8 0.0 copy-done.2
  40.8 0.0 copy-done
  40.8 19.3 %joint.1 = (f32[6,1280]{1,0:T(8,128)S(1)}, f32[6,1280]{1,0:T(8,128)S(1)}, f32[24,320]{1,0:T(8,128)S(1)}) custom-call(s32[4]{0:T(128)S(1)} %copy-done.1, bf16[24,640]{1,0:T(8,128)(2,1)S(1)} %bitcast.104, bf16[16,80,128]{2,1,0:T(8,128)(2,1)S(1)} %bitcast.102, bf16[6,80,128]{2,1,0:T(8,128)(2,1)S(1)} %copy-done, ...), custom_call_target="tpu_custom_call" | custom-call | flops 10066329600 | bytes 2097152 | tf_op jit(solution)/shard_map/joint/pallas_call | solution.py:192
  60.1 0.1 reshape.26
  60.2 0.1 reshape.25
  60.3 2.7 %collective-permute-start.7 = (f32[3,24,320]{2,1,0:T(8,128)S(1)}, f32[3,24,320]{2,1,0:T(8,128)S(1)}, u32[]{:S(2)}, u32[]{:S(2)}) collective-permute-start(f32[3,24,320]{2,1,0:T(8,128)S(1)} %pad_maximum_fusion), channel_id=1, source_target_pairs={{0,3},{1,0},{2,1},{3,2},{4,7},{5,4},{6,5},{7,6},{8,11},{9,8},{10,9... | collective-permute-start | bytes 276488 | tf_op jit(solution)/shard_map/combine_vocab/ppermute | solution.py:391
  62.9 0.3 collective-permute-start.6
  63.3 0.7 collective-permute-start.5
  65.3 0.1 reshape.27
  65.4 0.1 reshape.24
  65.4 0.0 collective-permute-done.7
  65.4 2.9 %collective-permute-done.6 = f32[3,24,320]{2,1,0:T(8,128)S(1)} collective-permute-done((f32[3,24,320]{2,1,0:T(8,128)S(1)}, f32[3,24,320]{2,1,0:T(8,128)S(1)}, u32[]{:S(2)}, u32[]{:S(2)}) %collective-permute-start.6) | collective-permute-done | bytes 92192 | tf_op jit(solution)/shard_map/combine_vocab/ppermute | solution.py:391
  68.4 3.4 %collective-permute-done.5 = f32[3,24,320]{2,1,0:T(8,128)S(1)} collective-permute-done((f32[3,24,320]{2,1,0:T(8,128)S(1)}, f32[3,24,320]{2,1,0:T(8,128)S(1)}, u32[]{:S(2)}, u32[]{:S(2)}) %collective-permute-start.5) | collective-permute-done | bytes 92192 | tf_op jit(solution)/shard_map/combine_vocab/ppermute | solution.py:391
  71.8 0.1 add_subtract_fusion
  71.8 0.1 fusion.1
  71.9 18.3 %all-gather.1 = f32[32,24,320]{2,1,0:T(8,128)S(1)} all-gather(f32[2,24,320]{2,1,0:T(8,128)S(1)} %pad_maximum_fusion.1), channel_id=3, replica_groups=mesh['batch'=4,'tm'=16,'label'=4] {'tm'}, dimensions={0}, use_global_device_ids=true | all-gather | bytes 1044480 | tf_op jit(solution)/shard_map/gather_grid/all_gather | solution.py:438
  90.2 9.3 %lattice.1 = f32[1,1]{1,0:T(1,128)} custom-call(s32[1]{0:T(128)S(6)} %copy.12.frame_len_ref, s32[1]{0:T(128)S(6)} %copy.13.label_len_ref, f32[16,2,24,320]{3,2,1,0:T(8,128)S(1)} %bitcast.99), custom_call_target="tpu_custom_call" | custom-call | tf_op jit(solution)/shard_map/lattice/pallas_call | solution.py:370
  99.6 0.7 fusion.14
  (8 shorter events, 0.1 us)
Async XLA Ops:
  1.2 39.5 %copy-start.1 = (s32[4]{0:T(128)S(1)}, s32[4]{0:T(128)}, u32[]{:S(2)}) copy-start(s32[4]{0:T(128)} %pad_add_fusion.place_ref) | copy-start | bytes 52
  1.2 39.5 %copy-start.2 = (bf16[1,24,640]{2,1,0:T(8,128)(2,1)S(1)}, bf16[1,24,640]{2,1,0:T(8,128)(2,1)}, u32[]{:S(2)}) copy-start(bf16[1,24,640]{2,1,0:T(8,128)(2,1)} %param.6) | copy-start | bytes 92164
  3.0 37.8 %copy-start = (bf16[6,80,128]{2,1,0:T(8,128)(2,1)S(1)}, bf16[6,80,128]{2,1,0:T(8,128)(2,1)}, u32[]{:S(2)}) copy-start(bf16[6,80,128]{2,1,0:T(8,128)(2,1)} %get-tuple-element.9.own_pred_ref) | copy-start | bytes 368644
  25.6 10.0 %collective-permute-start = (bf16[16,80,128]{2,1,0:T(8,128)(2,1)S(1)}, bf16[16,80,128]{2,1,0:T(8,128)(2,1)S(1)}, u32[]{:S(2)}, u32[]{:S(2)}) collective-permute-start(bf16[16,80,128]{2,1,0:T(8,128)(2,1)S(1)} %bitcast.100), channel_id=1, source_target_pairs={{0,64},{4,196},{8,72},{12,204},{16,80},{20,212},{24,88},{28,220},{... | collective-permute-start | bytes 983048 | tf_op jit(solution)/shard_map/fetch/ppermute | solution.py:411
  28.0 7.5 %collective-permute-start.1 = (bf16[8,80,128]{2,1,0:T(8,128)(2,1)S(1)}, bf16[8,80,128]{2,1,0:T(8,128)(2,1)S(1)}, u32[]{:S(2)}, u32[]{:S(2)}) collective-permute-start(bf16[8,80,128]{2,1,0:T(8,128)(2,1)S(1)} %constant_dynamic-slice_fusion.1), channel_id=1, source_target_pairs={{0,128},{4,132},{8,136},{12,140},{16,144},{20,148},{24,152},{28,15... | collective-permute-start | bytes 491528 | tf_op jit(solution)/shard_map/fetch/ppermute | solution.py:411
  28.7 7.0 %collective-permute-start.2 = (bf16[6,80,128]{2,1,0:T(8,128)(2,1)}, bf16[6,80,128]{2,1,0:T(8,128)(2,1)S(1)}, u32[]{:S(2)}, u32[]{:S(2)}) collective-permute-start(bf16[6,80,128]{2,1,0:T(8,128)(2,1)} %get-tuple-element.9.own_pred_ref), channel_id=1, source_target_pairs={{0,1},{4,7},{8,9},{12,15},{16,17},{20,23},{24,25},{28,31},{32,33},... | collective-permute-start | bytes 368648 | tf_op jit(solution)/shard_map/fetch/ppermute | solution.py:411
  32.3 5.5 %collective-permute-start.3 = (bf16[3,80,128]{2,1,0:T(8,128)(2,1)S(1)}, bf16[3,80,128]{2,1,0:T(8,128)(2,1)S(1)}, u32[]{:S(2)}, u32[]{:S(2)}) collective-permute-start(bf16[3,80,128]{2,1,0:T(8,128)(2,1)S(1)} %constant_dynamic-slice_fusion), channel_id=1, source_target_pairs={{0,2},{4,6},{8,10},{12,14},{16,18},{20,22},{24,26},{28,30},{32,34}... | collective-permute-start | bytes 184328 | tf_op jit(solution)/shard_map/fetch/ppermute | solution.py:411
  37.7 3.0 %collective-permute-start.4 = (bf16[33,80,128]{2,1,0:T(8,128)(2,1)S(1)}, bf16[33,80,128]{2,1,0:T(8,128)(2,1)S(1)}, u32[]{:S(2)}, u32[]{:S(2)}) collective-permute-start(bf16[33,80,128]{2,1,0:T(8,128)(2,1)S(1)} %constant_dynamic-update-slice_fusion.mine_ref), channel_id=1, source_target_pairs={{0,4},{4,0},{8,12},{12,8},{16,20},{20,16},{24,28},{28,24},{32,36},... | collective-permute-start | bytes 2027528 | tf_op jit(solution)/shard_map/fetch/ppermute | solution.py:425
  60.3 5.2 %collective-permute-start.7 = (f32[3,24,320]{2,1,0:T(8,128)S(1)}, f32[3,24,320]{2,1,0:T(8,128)S(1)}, u32[]{:S(2)}, u32[]{:S(2)}) collective-permute-start(f32[3,24,320]{2,1,0:T(8,128)S(1)} %pad_maximum_fusion), channel_id=1, source_target_pairs={{0,3},{1,0},{2,1},{3,2},{4,7},{5,4},{6,5},{7,6},{8,11},{9,8},{10,9... | collective-permute-start | bytes 276488 | tf_op jit(solution)/shard_map/combine_vocab/ppermute | solution.py:391
  62.9 5.4 %collective-permute-start.6 = (f32[3,24,320]{2,1,0:T(8,128)S(1)}, f32[3,24,320]{2,1,0:T(8,128)S(1)}, u32[]{:S(2)}, u32[]{:S(2)}) collective-permute-start(f32[3,24,320]{2,1,0:T(8,128)S(1)} %pad_maximum_fusion), channel_id=1, source_target_pairs={{0,2},{1,3},{2,0},{3,1},{4,6},{5,7},{6,4},{7,5},{8,10},{9,11},{10,... | collective-permute-start | bytes 276488 | tf_op jit(solution)/shard_map/combine_vocab/ppermute | solution.py:391
  63.3 8.5 %collective-permute-start.5 = (f32[3,24,320]{2,1,0:T(8,128)S(1)}, f32[3,24,320]{2,1,0:T(8,128)S(1)}, u32[]{:S(2)}, u32[]{:S(2)}) collective-permute-start(f32[3,24,320]{2,1,0:T(8,128)S(1)} %pad_maximum_fusion), channel_id=1, source_target_pairs={{0,1},{1,2},{2,3},{3,0},{4,5},{5,6},{6,7},{7,4},{8,9},{9,10},{10,1... | collective-permute-start | bytes 276488 | tf_op jit(solution)/shard_map/combine_vocab/ppermute | solution.py:391
where the time goes:
time: 100 us
  blocking collectives  40.9 us (41%)
  Pallas kernels  30.4 us (30%)
  waiting for transfers between devices  13.1 us (13%)
  starting transfers between devices  11.1 us (11%)
  between operations  2.02 us (2%)
  other arithmetic  1.43 us (1%)
  local copies, waits for them, and re-layouts  1.29 us (1%)
    all_gather x1, blocking collectives, shards(): own = lax.all_gather(own, 'tm', axis=0, tiled=False)  22.6 us
    pallas_call x1, Pallas kernels, joint_terms(): pl.pallas_call(joint_kernel, out_shape=(grouped, grouped, jax.ShapeDtypeS...  19.3 us
    all_gather x1, blocking collectives, shards(): lax.all_gather(jnp.stack([log_blank, log_label]), 'tm', axis=0, tiled=False)  18.3 us
    pallas_call x1, Pallas kernels, lattice_loss(): pl.pallas_call(lattice_kernel, out_shape=jax.ShapeDtypeStruct((1, 1), F32...  9.34 us
    ppermute x3, waiting for transfers between devices, around(): lax.ppermute(array, axis, [(i, (i + by) % size) for i in range(size)])  6.34 us
    ppermute x4, starting transfers between devices, both_ways(): return (lax.ppermute(array, axes, near), lax.ppermute(half, axes, opposite))  6.17 us
    ppermute x4, waiting for transfers between devices, both_ways(): return (lax.ppermute(array, axes, near), lax.ppermute(half, axes, opposite))  5.01 us
    ppermute x3, starting transfers between devices, around(): lax.ppermute(array, axis, [(i, (i + by) % size) for i in range(size)])  3.69 us
  transfers between devices with their start and end apart: 8, of which 5 were waited for; matrix products, arithmetic and copies ran while one was open for 1% of the time, Pallas kernels for 0%

commit v1 on v0

--- a/solution.py
+++ b/solution.py
@@ -10,15 +10,16 @@
 NEG = -1e30
 F32 = jnp.float32
 BF16 = jnp.bfloat16
-SPAN = 8
+SPAN = 16
+SIDE = 8
 GROUP = 4
 CHUNKS = 2
 LABEL_WAYS = 4
 BATCH_WAYS = 4
 
 
-def pack_kernel(place_ref, weight_ref, pred_ref, labels_ref, block_ref, packed_ref):
-    mine, odd_block = place_ref[0], lax.rem(place_ref[3], 2) == 1
+def pack_kernel(weight_ref, pred_ref, labels_ref, block_ref, packed_ref):
+    mine, odd_block = lax.axis_index("label"), lax.rem(lax.axis_index("tm"), 2) == 1
     tiles, positions, _ = packed_ref.shape
     rows = block_ref.shape[0]
     lane = lax.broadcasted_iota(jnp.int32, (rows, 128), 1)
@@ -41,7 +42,7 @@
     packed_ref[tiles - 1] = jnp.where(lane == 0, high, jnp.where(lane == 1, low, 0.0)).astype(BF16)
 
 
-def pack(place, weight, pred, labels):
+def pack(weight, pred, labels):
     positions, width = pred.shape
     vmem = pl.BlockSpec(memory_space=pltpu.VMEM)
     return pl.pallas_call(
@@ -50,18 +51,18 @@
             jax.ShapeDtypeStruct((weight.shape[0] // 2, 128), BF16),
             jax.ShapeDtypeStruct((width // 128 + 1, positions, 128), BF16),
         ),
-        in_specs=[pl.BlockSpec(memory_space=pltpu.SMEM)] + [vmem] * 3,
+        in_specs=[vmem] * 3,
         out_specs=(vmem, vmem),
         name="pack",
-    )(place, weight, pred, labels)
+    )(weight, pred, labels)
 
 
 def joint_kernel(
-    place_ref, enc_ref, own_ref, own_pred_ref, mine_ref, theirs_ref,
+    enc_ref, own_ref, own_pred_ref, mine_ref, theirs_ref,
     lse_ref, blank_ref, picked_ref,
     enc, pred, chosen, picks, columns_first, weight, hidden_a, hidden_b, logits_a, logits_b, top, total, top_a, top_b,
 ):
-    mine, batch, core = place_ref[0], place_ref[1], place_ref[2]
+    mine, batch, core = lax.axis_index("label"), lax.axis_index("batch"), lax.rem(lax.axis_index("tm"), 2)
     frames, width = enc_ref.shape
     tiles, positions, _ = pred.shape
     share = weight.shape[0]
@@ -179,7 +180,7 @@
     picked_ref[...] = picks[...].T[:frames, :]
 
 
-def joint_terms(place, enc, own, own_pred, mine, theirs):
+def joint_terms(enc, own, own_pred, mine, theirs):
     frames, width = enc.shape
     tiles = own_pred.shape[0]
     positions = LABEL_WAYS * own_pred.shape[1]
@@ -192,7 +193,7 @@
     return pl.pallas_call(
         joint_kernel,
         out_shape=(grouped, grouped, jax.ShapeDtypeStruct((frames, positions), F32)),
-        in_specs=[smem] + [vmem] * 5,
+        in_specs=[vmem] * 5,
         out_specs=(vmem,) * 3,
         scratch_shapes=[
             pltpu.VMEM((frames, width), F32),
@@ -213,7 +214,7 @@
         compiler_params=pltpu.CompilerParams(vmem_limit_bytes=48 << 20),
         cost_estimate=pl.CostEstimate(flops=flops, bytes_accessed=2 << 20, transcendentals=0),
         name="joint",
-    )(place, enc, own, own_pred, mine, theirs)
+    )(enc, own, own_pred, mine, theirs)
 
 
 def tree(combine, terms):
@@ -233,9 +234,21 @@
     return top + jnp.log(tree(jnp.add, [jnp.exp(term - top) for term in terms]))
 
 
+def strips_of(values):
+    return [values[:, start:start + 128] for start in range(0, values.shape[1], 128)]
+
+
+def merge(strips, crossed, step):
+    parts = [jnp.where(crossed, strips[(p - step) % len(strips)], strips[p]) for p in range(len(strips))]
+    return jnp.concatenate(parts, axis=1)
+
+
 def shift_lanes(values, by):
-    by = by % values.shape[1]
-    return values if by == 0 else pltpu.roll(values, by, 1)
+    if by == 0:
+        return values
+    lane = lax.broadcasted_iota(jnp.int32, (values.shape[0], 128), 1)
+    turned = [pltpu.roll(strip, by % 128, 1) for strip in strips_of(values)]
+    return merge(turned, lane < by, 1) if by > 0 else merge(turned, lane >= 128 + by, -1)
 
 
 def compose(first, then):
@@ -261,7 +274,7 @@
 
 
 def lattice_kernel(
-    frame_len_ref, label_len_ref, grid_ref, loss_ref, stay, move, ahead, back, ahead_far, back_far
+    frame_len_ref, label_len_ref, grid_ref, loss_ref, blank_ref, label_ref, stay, move, ahead, back, ahead_far, back_far
 ):
     blocks, _, frames_dev, positions = grid_ref.shape
     frames = blocks * frames_dev
@@ -269,6 +282,13 @@
     lanes_all = 128 * strips
     flen = frame_len_ref[0]
     ulen = label_len_ref[0]
+    mine, held = lax.axis_index("label"), blank_ref.shape[1]
+    for which, ref in enumerate((blank_ref, label_ref)):
+        rows = grid_ref[lax.axis_index("tm"), which]
+        own = rows[:, :held]
+        for index in range(1, LABEL_WAYS):
+            own = jnp.where(mine == index, rows[:, index * held:(index + 1) * held], own)
+        ref[...] = own
     spare = jnp.full((frames, lanes_all - positions), NEG, F32)
     tall = frames + 128
     pad = jnp.full((tall - frames, 128), NEG, F32)
@@ -288,20 +308,20 @@
             strip = jnp.concatenate([source[:, start:start + 128], pad], axis=0)
             out[part, start:start + rows, :] = shear(strip, lead)[:rows]
 
-    depth = SPAN * SPAN
+    depth = SIDE * SPAN
     for group in range(diagonals // depth):
         base = group * depth
         live = [p for p in range(strips) if 128 * p <= base + depth and base < 128 * p + 128 + frames]
         first, count_live = live[0], len(live)
-        row = lax.broadcasted_iota(jnp.int32, (SPAN, 128 * count_live), 0)
-        lane = lax.broadcasted_iota(jnp.int32, (SPAN, 128 * count_live), 1) + 128 * first
+        row = lax.broadcasted_iota(jnp.int32, (SIDE, 128 * count_live), 0)
+        lane = lax.broadcasted_iota(jnp.int32, (SIDE, 128 * count_live), 1) + 128 * first
         in_row = lane < positions
         moves_in = in_row & (lane > 0)
         rest = jnp.where(lane == ulen, 0.0, NEG)
         steps = []
         for step in range(SPAN):
             time = base + row * SPAN + step - lane
-            at = pl.ds(base + step, SPAN, stride=SPAN)
+            at = pl.ds(base + step, SIDE, stride=SPAN)
             held = jnp.concatenate([stay[part, at, :] for part in live], axis=1)
             moved = jnp.concatenate([move[part, at, :] for part in live], axis=1)
             held = jnp.where(in_row & (time < flen), held, rest)
@@ -309,7 +329,7 @@
             steps.append([held, moved])
         while len(steps) > 1:
             steps = [compose(steps[i], steps[i + 1]) for i in range(0, len(steps), 2)]
-        at = group * SPAN
+        at = group * SIDE
         for count, values in enumerate(steps[0]):
             moved = shift_lanes(values, -count)
             for part in range(strips):
@@ -317,35 +337,42 @@
                     strip = slice(128 * (part - first), 128 * (part - first) + 128)
                     forth, from_back = values[:, strip], moved[:, strip]
                 else:
-                    forth = jnp.full((SPAN, 128), NEG, F32)
+                    forth = jnp.full((SIDE, 128), NEG, F32)
                     if count == 0:
-                        lane = lax.broadcasted_iota(jnp.int32, (SPAN, 128), 1) + 128 * part
+                        lane = lax.broadcasted_iota(jnp.int32, (SIDE, 128), 1) + 128 * part
                         forth = jnp.where(lane == ulen, 0.0, NEG)
                     from_back = forth
                 if count < SPAN:
-                    ahead[part, pl.ds(at * SPAN + count, SPAN, stride=SPAN), :] = forth
-                    back[part, pl.ds(at * SPAN + SPAN - 1 - count, SPAN, stride=SPAN), :] = from_back
+                    ahead[part, pl.ds(at * SPAN + count, SIDE, stride=SPAN), :] = forth
+                    back[part, pl.ds(at * SPAN + SPAN - 1 - count, SIDE, stride=SPAN), :] = from_back
                 else:
-                    ahead_far[at:at + SPAN, 128 * part:128 * part + 128] = forth
-                    back_far[at:at + SPAN, 128 * part:128 * part + 128] = from_back
+                    ahead_far[at:at + SIDE, 128 * part:128 * part + 128] = forth
+                    back_far[at:at + SIDE, 128 * part:128 * part + 128] = from_back
 
     spans = diagonals // SPAN
     place = lax.broadcasted_iota(jnp.int32, (1, lanes_all), 1)
 
-    def advance(state, shift, table, far, block, far_shift):
+    def advance(state, step, table, far, block):
         rows = pl.ds(pl.multiple_of(block * SPAN, SPAN), SPAN)
         weights = jnp.concatenate([table[part, rows, :] for part in range(strips)], axis=1)
-        spread = jnp.broadcast_to(state, (SPAN, lanes_all))
-        near = weights + pltpu.roll(spread, shift, 1, stride=1, stride_axis=0)
-        last = far[pl.ds(block, 1), :] + shift_lanes(state, far_shift)
+        first = 0 if step > 0 else 128 - SPAN + 1
+        turned = [
+            pltpu.roll(jnp.broadcast_to(strip, (SPAN, 128)), first, 1, stride=1, stride_axis=0)
+            for strip in strips_of(state)
+        ]
+        lane = lax.broadcasted_iota(jnp.int32, (SPAN, 128), 1)
+        row = lax.broadcasted_iota(jnp.int32, (SPAN, 128), 0)
+        crossed = lane < row if step > 0 else lane >= first + row
+        near = weights + merge(turned, crossed, step)
+        last = far[pl.ds(block, 1), :] + shift_lanes(state, step * SPAN)
         top = jnp.maximum(jnp.max(near, axis=0, keepdims=True), last)
         total = jnp.sum(jnp.exp(near - top), axis=0, keepdims=True) + jnp.exp(last - top)
         return top + jnp.log(total)
 
     def sweep(index, carry):
         alpha, beta = carry
-        alpha = advance(alpha, 0, ahead, ahead_far, index, SPAN)
-        beta = advance(beta, lanes_all - SPAN + 1, back, back_far, spans - 1 - index, -SPAN)
+        alpha = advance(alpha, 1, ahead, ahead_far, index)
+        beta = advance(beta, -1, back, back_far, spans - 1 - index)
         return alpha, beta
 
     alpha = jnp.where(place == 0, 0.0, NEG)
@@ -360,18 +387,19 @@
 def lattice_loss(frame_len, label_len, grid):
     blocks, _, frames_dev, positions = grid.shape
     lanes = -(-positions // 128) * 128
-    diagonals = -(-(blocks * frames_dev + positions) // (SPAN * SPAN)) * SPAN * SPAN
+    diagonals = -(-(blocks * frames_dev + positions) // (SIDE * SPAN)) * SIDE * SPAN
     assert (diagonals // SPAN) % 2 == 0
     strip = pltpu.VMEM((lanes // 128, diagonals, 128), F32)
+    block = jax.ShapeDtypeStruct((frames_dev, positions // LABEL_WAYS), F32)
     table = pltpu.VMEM((lanes // 128, diagonals, 128), F32)
     far = pltpu.VMEM((diagonals // SPAN, lanes), F32)
     vmem = pl.BlockSpec(memory_space=pltpu.VMEM)
     smem = pl.BlockSpec(memory_space=pltpu.SMEM)
     return pl.pallas_call(
         lattice_kernel,
-        out_shape=jax.ShapeDtypeStruct((1, 1), F32),
+        out_shape=(jax.ShapeDtypeStruct((1, 1), F32), block, block),
         in_specs=[smem, smem, vmem],
-        out_specs=vmem,
+        out_specs=(vmem,) * 3,
         scratch_shapes=[
             strip,
             strip,
@@ -389,7 +417,7 @@
     size = lax.axis_size(axis)
     moved = [
         lax.ppermute(array, axis, [(i, (i + by) % size) for i in range(size)])
-        for by in range(1, size)
+        for by in range(size - 1, 0, -1)
     ]
     return [array] + moved
 
@@ -412,18 +440,15 @@
 
 
 def shards(enc_joint, pred_joint, out_weight, labels, frame_len, label_len):
-    positions = pred_joint.shape[1]
     mine = lax.axis_index("label")
-    here = lax.axis_index("tm")
-    place = jnp.stack([mine, lax.axis_index("batch"), here % 2, here]).astype(jnp.int32)
-    own, own_pred = pack(place, out_weight, pred_joint[0], labels)
+    own, own_pred = pack(out_weight, pred_joint[0], labels)
     with jax.named_scope("gather_weight"):
         own = lax.all_gather(own, "tm", axis=0, tiled=False)
     with jax.named_scope("fetch"):
         from_others = jnp.concatenate([*both_ways(own, "batch"), *both_ways(own_pred, "label")], axis=0)
         swap = [(i, i ^ 1) for i in range(lax.axis_size("tm"))]
         theirs = lax.ppermute(from_others, "tm", swap)
-    lse, blank, picked = joint_terms(place, enc_joint[0], own, own_pred, from_others, theirs)
+    lse, blank, picked = joint_terms(enc_joint[0], own, own_pred, from_others, theirs)
     with jax.named_scope("combine_vocab"):
         blank = jnp.where(mine == 0, blank, 0.0)
         parts = jnp.stack([lse.reshape(picked.shape), blank.reshape(picked.shape), picked])
@@ -432,12 +457,10 @@
         norm = top + jnp.log(sum(jnp.exp(part[0] - top) for part in parts))
         log_blank = sum(part[1] for part in parts) - norm
         log_label = sum(part[2] for part in parts) - norm
-    out_blank = lax.dynamic_slice_in_dim(log_blank, mine * positions, positions, axis=1)
-    out_label = lax.dynamic_slice_in_dim(log_label, mine * positions, positions, axis=1)
     with jax.named_scope("gather_grid"):
         grid = lax.all_gather(jnp.stack([log_blank, log_label]), "tm", axis=0, tiled=False)
-    loss = lattice_loss(frame_len, label_len, grid).reshape(1)
-    return out_blank[None], out_label[None], loss
+    loss, out_blank, out_label = lattice_loss(frame_len, label_len, grid)
+    return out_blank[None], out_label[None], loss.reshape(1)
 
 
 def solution(mesh):

time: 100 us -> 97.7 us (0.977)
  Pallas kernels: 30.4 us -> 28.9 us
  other arithmetic: 1.43 us -> 0.14 us
where the time goes in v1:
time: 97.7 us; the launch traced here: 97.5 us
  blocking collectives  40.9 us (42%)
  Pallas kernels  28.9 us (30%)
  waiting for transfers between devices  13.2 us (14%)
  starting transfers between devices  11.2 us (11%)
  between operations  2.01 us (2%)
  local copies, waits for them, and re-layouts  1.21 us (1%)
    all_gather x1, blocking collectives, shards(): own = lax.all_gather(own, 'tm', axis=0, tiled=False)  22.6 us
    pallas_call x1, Pallas kernels, joint_terms(): pl.pallas_call(joint_kernel, out_shape=(grouped, grouped, jax.ShapeDtypeS...  18.8 us
    all_gather x1, blocking collectives, shards(): lax.all_gather(jnp.stack([log_blank, log_label]), 'tm', axis=0, tiled=False)  18.3 us
    pallas_call x1, Pallas kernels, lattice_loss(): pl.pallas_call(lattice_kernel, out_shape=(jax.ShapeDtypeStruct((1, 1), F3...  8.36 us
    ppermute x3, waiting for transfers between devices, around(): lax.ppermute(array, axis, [(i, (i + by) % size) for i in range(size)])  6.43 us
    ppermute x4, starting transfers between devices, both_ways(): return (lax.ppermute(array, axes, near), lax.ppermute(half, axes, opposite))  6.17 us
    ppermute x4, waiting for transfers between devices, both_ways(): return (lax.ppermute(array, axes, near), lax.ppermute(half, axes, opposite))  5.01 us
    ppermute x3, starting transfers between devices, around(): lax.ppermute(array, axis, [(i, (i + by) % size) for i in range(size)])  3.71 us
  transfers between devices with their start and end apart: 8, of which 5 were waited for; matrix products, arithmetic and copies ran while one was open for 1% of the time, Pallas kernels for 0%

profile of v1, /device:TPU:1, one launch (start us, length us, event | category | flops | bytes accessed | tf_op | source)
XLA Modules:
  0.0 97.5 jit_solution(11261747455674115471)
XLA Ops:
  0.6 0.0 copy-start.1
  0.6 1.7 %pack.1 = (bf16[80,128]{1,0:T(8,128)(2,1)}, bf16[6,80,128]{2,1,0:T(8,128)(2,1)}) custom-call(bf16[160,256]{1,0:T(8,128)(2,1)} %weight_ref.1, bf16[80,640]{1,0:T(8,128)(2,1)} %bitcast.95, s32[1,80]{1,0:T(1,128)} %labels_ref.1), custom_call_target="tpu_custom_call" | custom-call | tf_op jit(solution)/shard_map/pack/pallas_call | solution.py:48
  2.4 0.0 copy-start
  2.4 22.6 %all-gather = bf16[1280,128]{1,0:T(8,128)(2,1)S(1)} all-gather(bf16[80,128]{1,0:T(8,128)(2,1)} %get-tuple-element.11), channel_id=2, replica_groups=mesh['batch'=4,'tm'=16,'label'=4] {'tm'}, dimensions={0}, use_global_device_ids=true | all-gather | bytes 348160 | tf_op jit(solution)/shard_map/gather_weight/all_gather | solution.py:446
  24.9 2.5 %collective-permute-start = (bf16[16,80,128]{2,1,0:T(8,128)(2,1)S(1)}, bf16[16,80,128]{2,1,0:T(8,128)(2,1)S(1)}, u32[]{:S(2)}, u32[]{:S(2)}) collective-permute-start(bf16[16,80,128]{2,1,0:T(8,128)(2,1)S(1)} %bitcast.90), channel_id=1, source_target_pairs={{0,64},{4,196},{8,72},{12,204},{16,80},{20,212},{24,88},{28,220},{... | collective-permute-start | bytes 983048 | tf_op jit(solution)/shard_map/fetch/ppermute | solution.py:439
  27.4 0.6 collective-permute-start.1
  28.0 2.7 %collective-permute-start.2 = (bf16[6,80,128]{2,1,0:T(8,128)(2,1)}, bf16[6,80,128]{2,1,0:T(8,128)(2,1)S(1)}, u32[]{:S(2)}, u32[]{:S(2)}) collective-permute-start(bf16[6,80,128]{2,1,0:T(8,128)(2,1)} %get-tuple-element.12.own_pred_ref), channel_id=1, source_target_pairs={{0,1},{4,7},{8,9},{12,15},{16,17},{20,23},{24,25},{28,31},{32,33},... | collective-permute-start | bytes 368648 | tf_op jit(solution)/shard_map/fetch/ppermute | solution.py:439
  30.8 0.9 constant_dynamic-slice_fusion
  31.6 0.3 collective-permute-start.3
  32.0 3.0 %collective-permute-done = bf16[16,80,128]{2,1,0:T(8,128)(2,1)S(1)} collective-permute-done((bf16[16,80,128]{2,1,0:T(8,128)(2,1)S(1)}, bf16[16,80,128]{2,1,0:T(8,128)(2,1)S(1)}, u32[]{:S(2)}, u32[]{:S(2)}) %collective-permute-start) | collective-permute-done | bytes 327712 | tf_op jit(solution)/shard_map/fetch/ppermute | solution.py:439
  35.0 0.0 collective-permute-done.1
  35.0 0.0 collective-permute-done.2
  35.1 2.1 %collective-permute-done.3 = bf16[3,80,128]{2,1,0:T(8,128)(2,1)S(1)} collective-permute-done((bf16[3,80,128]{2,1,0:T(8,128)(2,1)S(1)}, bf16[3,80,128]{2,1,0:T(8,128)(2,1)S(1)}, u32[]{:S(2)}, u32[]{:S(2)}) %collective-permute-start.3) | collective-permute-done | bytes 61472 | tf_op jit(solution)/shard_map/fetch/ppermute | solution.py:439
  37.1 1.3 %collective-permute-start.4 = (bf16[33,80,128]{2,1,0:T(8,128)(2,1)S(1)}, bf16[33,80,128]{2,1,0:T(8,128)(2,1)S(1)}, u32[]{:S(2)}, u32[]{:S(2)}) collective-permute-start(bf16[33,80,128]{2,1,0:T(8,128)(2,1)S(1)} %constant_dynamic-update-slice_fusion.mine_ref), channel_id=1, source_target_pairs={{0,4},{4,0},{8,12},{12,8},{16,20},{20,16},{24,28},{28,24},{32,36},... | collective-permute-start | bytes 2027528 | tf_op jit(solution)/shard_map/fetch/ppermute | solution.py:450
  38.4 1.8 %collective-permute-done.4.theirs_ref = bf16[33,80,128]{2,1,0:T(8,128)(2,1)S(1)} collective-permute-done((bf16[33,80,128]{2,1,0:T(8,128)(2,1)S(1)}, bf16[33,80,128]{2,1,0:T(8,128)(2,1)S(1)}, u32[]{:S(2)}, u32[]{:S(2)}) %collective-permute-start.4) | collective-permute-done | bytes 675872 | tf_op jit(solution)/shard_map/fetch/ppermute | solution.py:450
  40.1 0.0 copy-done.1
  40.1 0.0 copy-done
  40.1 18.8 %joint.1 = (f32[6,1280]{1,0:T(8,128)S(1)}, f32[6,1280]{1,0:T(8,128)S(1)}, f32[24,320]{1,0:T(8,128)S(1)}) custom-call(bf16[24,640]{1,0:T(8,128)(2,1)S(1)} %bitcast.94, bf16[16,80,128]{2,1,0:T(8,128)(2,1)S(1)} %bitcast.92, bf16[6,80,128]{2,1,0:T(8,128)(2,1)S(1)} %copy-done, bf16[33,80,128]{2,1,0:T(8,128)(2,1)S(1)} %constant_dynamic-update-slice_fusion.mine_ref, ...), custom_call_target="tpu_custom_call" | custom-call | flops 10066329600 | bytes 2097152 | tf_op jit(solution)/shard_map/joint/pallas_call | solution.py:193
  59.0 0.1 reshape.22
  59.0 0.1 reshape.23
  59.1 2.7 %collective-permute-start.5 = (f32[3,24,320]{2,1,0:T(8,128)S(1)}, f32[3,24,320]{2,1,0:T(8,128)S(1)}, u32[]{:S(2)}, u32[]{:S(2)}) collective-permute-start(f32[3,24,320]{2,1,0:T(8,128)S(1)} %pad_maximum_fusion), channel_id=1, source_target_pairs={{0,3},{1,0},{2,1},{3,2},{4,7},{5,4},{6,5},{7,6},{8,11},{9,8},{10,9... | collective-permute-start | bytes 276488 | tf_op jit(solution)/shard_map/combine_vocab/ppermute | solution.py:419
  61.8 0.3 collective-permute-start.6
  62.2 0.7 collective-permute-start.7
  64.2 0.1 reshape.24
  64.2 0.0 collective-permute-done.5
  64.2 3.0 %collective-permute-done.6 = f32[3,24,320]{2,1,0:T(8,128)S(1)} collective-permute-done((f32[3,24,320]{2,1,0:T(8,128)S(1)}, f32[3,24,320]{2,1,0:T(8,128)S(1)}, u32[]{:S(2)}, u32[]{:S(2)}) %collective-permute-start.6) | collective-permute-done | bytes 92192 | tf_op jit(solution)/shard_map/combine_vocab/ppermute | solution.py:419
  67.3 3.4 %collective-permute-done.7 = f32[3,24,320]{2,1,0:T(8,128)S(1)} collective-permute-done((f32[3,24,320]{2,1,0:T(8,128)S(1)}, f32[3,24,320]{2,1,0:T(8,128)S(1)}, u32[]{:S(2)}, u32[]{:S(2)}) %collective-permute-start.7) | collective-permute-done | bytes 92192 | tf_op jit(solution)/shard_map/combine_vocab/ppermute | solution.py:419
  70.7 0.1 fusion.5
  70.7 0.1 fusion.2
  70.8 18.3 %all-gather.1 = f32[32,24,320]{2,1,0:T(8,128)S(1)} all-gather(f32[2,24,320]{2,1,0:T(8,128)S(1)} %pad_maximum_fusion.1), channel_id=3, replica_groups=mesh['batch'=4,'tm'=16,'label'=4] {'tm'}, dimensions={0}, use_global_device_ids=true | all-gather | bytes 1044480 | tf_op jit(solution)/shard_map/gather_grid/all_gather | solution.py:461
  89.1 8.4 %lattice.1 = (f32[1,1]{1,0:T(1,128)}, f32[24,80]{1,0:T(8,128)}, f32[24,80]{1,0:T(8,128)}) custom-call(s32[1]{0:T(128)S(6)} %copy.12.frame_len_ref, s32[1]{0:T(128)S(6)} %copy.13.label_len_ref, f32[16,2,24,320]{3,2,1,0:T(8,128)S(1)} %bitcast.89), custom_call_target="tpu_custom_call" | custom-call | tf_op jit(solution)/shard_map/lattice/pallas_call | solution.py:398
  (8 shorter events, 0.1 us)
Async XLA Ops:
  0.6 39.5 %copy-start.1 = (bf16[1,24,640]{2,1,0:T(8,128)(2,1)S(1)}, bf16[1,24,640]{2,1,0:T(8,128)(2,1)}, u32[]{:S(2)}) copy-start(bf16[1,24,640]{2,1,0:T(8,128)(2,1)} %param.6) | copy-start | bytes 92164
  2.4 37.8 %copy-start = (bf16[6,80,128]{2,1,0:T(8,128)(2,1)S(1)}, bf16[6,80,128]{2,1,0:T(8,128)(2,1)}, u32[]{:S(2)}) copy-start(bf16[6,80,128]{2,1,0:T(8,128)(2,1)} %get-tuple-element.12.own_pred_ref) | copy-start | bytes 368644
  24.9 10.0 %collective-permute-start = (bf16[16,80,128]{2,1,0:T(8,128)(2,1)S(1)}, bf16[16,80,128]{2,1,0:T(8,128)(2,1)S(1)}, u32[]{:S(2)}, u32[]{:S(2)}) collective-permute-start(bf16[16,80,128]{2,1,0:T(8,128)(2,1)S(1)} %bitcast.90), channel_id=1, source_target_pairs={{0,64},{4,196},{8,72},{12,204},{16,80},{20,212},{24,88},{28,220},{... | collective-permute-start | bytes 983048 | tf_op jit(solution)/shard_map/fetch/ppermute | solution.py:439
  27.4 7.5 %collective-permute-start.1 = (bf16[8,80,128]{2,1,0:T(8,128)(2,1)S(1)}, bf16[8,80,128]{2,1,0:T(8,128)(2,1)S(1)}, u32[]{:S(2)}, u32[]{:S(2)}) collective-permute-start(bf16[8,80,128]{2,1,0:T(8,128)(2,1)S(1)} %constant_dynamic-slice_fusion.1), channel_id=1, source_target_pairs={{0,128},{4,132},{8,136},{12,140},{16,144},{20,148},{24,152},{28,15... | collective-permute-start | bytes 491528 | tf_op jit(solution)/shard_map/fetch/ppermute | solution.py:439
  28.0 7.0 %collective-permute-start.2 = (bf16[6,80,128]{2,1,0:T(8,128)(2,1)}, bf16[6,80,128]{2,1,0:T(8,128)(2,1)S(1)}, u32[]{:S(2)}, u32[]{:S(2)}) collective-permute-start(bf16[6,80,128]{2,1,0:T(8,128)(2,1)} %get-tuple-element.12.own_pred_ref), channel_id=1, source_target_pairs={{0,1},{4,7},{8,9},{12,15},{16,17},{20,23},{24,25},{28,31},{32,33},... | collective-permute-start | bytes 368648 | tf_op jit(solution)/shard_map/fetch/ppermute | solution.py:439
  31.6 5.5 %collective-permute-start.3 = (bf16[3,80,128]{2,1,0:T(8,128)(2,1)S(1)}, bf16[3,80,128]{2,1,0:T(8,128)(2,1)S(1)}, u32[]{:S(2)}, u32[]{:S(2)}) collective-permute-start(bf16[3,80,128]{2,1,0:T(8,128)(2,1)S(1)} %constant_dynamic-slice_fusion), channel_id=1, source_target_pairs={{0,2},{4,6},{8,10},{12,14},{16,18},{20,22},{24,26},{28,30},{32,34}... | collective-permute-start | bytes 184328 | tf_op jit(solution)/shard_map/fetch/ppermute | solution.py:439
  37.1 3.0 %collective-permute-start.4 = (bf16[33,80,128]{2,1,0:T(8,128)(2,1)S(1)}, bf16[33,80,128]{2,1,0:T(8,128)(2,1)S(1)}, u32[]{:S(2)}, u32[]{:S(2)}) collective-permute-start(bf16[33,80,128]{2,1,0:T(8,128)(2,1)S(1)} %constant_dynamic-update-slice_fusion.mine_ref), channel_id=1, source_target_pairs={{0,4},{4,0},{8,12},{12,8},{16,20},{20,16},{24,28},{28,24},{32,36},... | collective-permute-start | bytes 2027528 | tf_op jit(solution)/shard_map/fetch/ppermute | solution.py:450
  59.1 5.1 %collective-permute-start.5 = (f32[3,24,320]{2,1,0:T(8,128)S(1)}, f32[3,24,320]{2,1,0:T(8,128)S(1)}, u32[]{:S(2)}, u32[]{:S(2)}) collective-permute-start(f32[3,24,320]{2,1,0:T(8,128)S(1)} %pad_maximum_fusion), channel_id=1, source_target_pairs={{0,3},{1,0},{2,1},{3,2},{4,7},{5,4},{6,5},{7,6},{8,11},{9,8},{10,9... | collective-permute-start | bytes 276488 | tf_op jit(solution)/shard_map/combine_vocab/ppermute | solution.py:419
  61.8 5.5 %collective-permute-start.6 = (f32[3,24,320]{2,1,0:T(8,128)S(1)}, f32[3,24,320]{2,1,0:T(8,128)S(1)}, u32[]{:S(2)}, u32[]{:S(2)}) collective-permute-start(f32[3,24,320]{2,1,0:T(8,128)S(1)} %pad_maximum_fusion), channel_id=1, source_target_pairs={{0,2},{1,3},{2,0},{3,1},{4,6},{5,7},{6,4},{7,5},{8,10},{9,11},{10,... | collective-permute-start | bytes 276488 | tf_op jit(solution)/shard_map/combine_vocab/ppermute | solution.py:419
  62.2 8.5 %collective-permute-start.7 = (f32[3,24,320]{2,1,0:T(8,128)S(1)}, f32[3,24,320]{2,1,0:T(8,128)S(1)}, u32[]{:S(2)}, u32[]{:S(2)}) collective-permute-start(f32[3,24,320]{2,1,0:T(8,128)S(1)} %pad_maximum_fusion), channel_id=1, source_target_pairs={{0,1},{1,2},{2,3},{3,0},{4,5},{5,6},{6,7},{7,4},{8,9},{9,10},{10,1... | collective-permute-start | bytes 276488 | tf_op jit(solution)/shard_map/combine_vocab/ppermute | solution.py:419

commit v2 on v1

--- a/solution.py
+++ b/solution.py
@@ -417,7 +417,7 @@
     size = lax.axis_size(axis)
     moved = [
         lax.ppermute(array, axis, [(i, (i + by) % size) for i in range(size)])
-        for by in range(size - 1, 0, -1)
+        for by in range(1, size)
     ]
     return [array] + moved
 
@@ -453,10 +453,12 @@
         blank = jnp.where(mine == 0, blank, 0.0)
         parts = jnp.stack([lse.reshape(picked.shape), blank.reshape(picked.shape), picked])
         parts = around(parts, "label")
-        top = functools.reduce(jnp.maximum, [part[0] for part in parts])
-        norm = top + jnp.log(sum(jnp.exp(part[0] - top) for part in parts))
-        log_blank = sum(part[1] for part in parts) - norm
-        log_label = sum(part[2] for part in parts) - norm
+        norm, log_blank, log_label = parts[0]
+        for part in parts[1:]:
+            norm = jnp.logaddexp(norm, part[0])
+            log_blank, log_label = log_blank + part[1], log_label + part[2]
+            norm, log_blank, log_label = lax.optimization_barrier((norm, log_blank, log_label))
+        log_blank, log_label = log_blank - norm, log_label - norm
     with jax.named_scope("gather_grid"):
         grid = lax.all_gather(jnp.stack([log_blank, log_label]), "tm", axis=0, tiled=False)
     loss, out_blank, out_label = lattice_loss(frame_len, label_len, grid)

time: 97.7 us -> 97 us (level)
  waiting for transfers between devices: 13.2 us -> 10.4 us
  starting transfers between devices: 11.2 us -> 12.4 us
    ppermute x3, waiting for transfers between devices: 6.43 us -> 3.61 us  [around(): lax.ppermute(array, axis, [(i, (i + by) % size) for i in range(size)])]
    ppermute x3, starting transfers between devices: 3.71 us -> 4.94 us  [around(): lax.ppermute(array, axis, [(i, (i + by) % size) for i in range(size)])]
where the time goes in v2:
time: 97 us; the launch traced here: 96.8 us
  blocking collectives  41.7 us (43%)
  Pallas kernels  28.9 us (30%)
  starting transfers between devices  12.4 us (13%)
  waiting for transfers between devices  10.4 us (11%)
  between operations  2.02 us (2%)
  local copies, waits for them, and re-layouts  1.29 us (1%)
    all_gather x1, blocking collectives, shards(): own = lax.all_gather(own, 'tm', axis=0, tiled=False)  22.6 us
    all_gather x1, blocking collectives, shards(): lax.all_gather(jnp.stack([log_blank, log_label]), 'tm', axis=0, tiled=False)  19.1 us
    pallas_call x1, Pallas kernels, joint_terms(): pl.pallas_call(joint_kernel, out_shape=(grouped, grouped, jax.ShapeDtypeS...  18.8 us
    pallas_call x1, Pallas kernels, lattice_loss(): pl.pallas_call(lattice_kernel, out_shape=(jax.ShapeDtypeStruct((1, 1), F3...  8.36 us
    ppermute x4, starting transfers between devices, both_ways(): return (lax.ppermute(array, axes, near), lax.ppermute(half, axes, opposite))  6.17 us
    ppermute x4, waiting for transfers between devices, both_ways(): return (lax.ppermute(array, axes, near), lax.ppermute(half, axes, opposite))  5.01 us
    ppermute x3, starting transfers between devices, around(): lax.ppermute(array, axis, [(i, (i + by) % size) for i in range(size)])  4.94 us
    ppermute x3, waiting for transfers between devices, around(): lax.ppermute(array, axis, [(i, (i + by) % size) for i in range(size)])  3.61 us
  transfers between devices with their start and end apart: 8, of which 5 were waited for; matrix products, arithmetic and copies ran while one was open for 1% of the time, Pallas kernels for 0%

profile of v2, /device:TPU:1, one launch (start us, length us, event | category | flops | bytes accessed | tf_op | source)
XLA Modules:
  0.0 96.8 jit_solution(17377419905862351638)
XLA Ops:
  0.6 0.0 copy-start.1
  0.6 1.7 %pack.1 = (bf16[80,128]{1,0:T(8,128)(2,1)}, bf16[6,80,128]{2,1,0:T(8,128)(2,1)}) custom-call(bf16[160,256]{1,0:T(8,128)(2,1)} %weight_ref.1, bf16[80,640]{1,0:T(8,128)(2,1)} %bitcast.54, s32[1,80]{1,0:T(1,128)} %labels_ref.1), custom_call_target="tpu_custom_call" | custom-call | tf_op jit(solution)/shard_map/pack/pallas_call | solution.py:48
  2.4 0.0 copy-start
  2.4 22.6 %all-gather = bf16[1280,128]{1,0:T(8,128)(2,1)S(1)} all-gather(bf16[80,128]{1,0:T(8,128)(2,1)} %get-tuple-element.20), channel_id=2, replica_groups=mesh['batch'=4,'tm'=16,'label'=4] {'tm'}, dimensions={0}, use_global_device_ids=true | all-gather | bytes 348160 | tf_op jit(solution)/shard_map/gather_weight/all_gather | solution.py:446
  24.9 2.5 %collective-permute-start = (bf16[16,80,128]{2,1,0:T(8,128)(2,1)S(1)}, bf16[16,80,128]{2,1,0:T(8,128)(2,1)S(1)}, u32[]{:S(2)}, u32[]{:S(2)}) collective-permute-start(bf16[16,80,128]{2,1,0:T(8,128)(2,1)S(1)} %bitcast.49), channel_id=1, source_target_pairs={{0,64},{4,196},{8,72},{12,204},{16,80},{20,212},{24,88},{28,220},{... | collective-permute-start | bytes 983048 | tf_op jit(solution)/shard_map/fetch/ppermute | solution.py:439
  27.4 0.6 collective-permute-start.1
  28.0 2.7 %collective-permute-start.2 = (bf16[6,80,128]{2,1,0:T(8,128)(2,1)}, bf16[6,80,128]{2,1,0:T(8,128)(2,1)S(1)}, u32[]{:S(2)}, u32[]{:S(2)}) collective-permute-start(bf16[6,80,128]{2,1,0:T(8,128)(2,1)} %get-tuple-element.21.own_pred_ref), channel_id=1, source_target_pairs={{0,1},{4,7},{8,9},{12,15},{16,17},{20,23},{24,25},{28,31},{32,33},... | collective-permute-start | bytes 368648 | tf_op jit(solution)/shard_map/fetch/ppermute | solution.py:439
  30.8 0.9 constant_dynamic-slice_fusion
  31.6 0.3 collective-permute-start.3
  32.0 3.0 %collective-permute-done = bf16[16,80,128]{2,1,0:T(8,128)(2,1)S(1)} collective-permute-done((bf16[16,80,128]{2,1,0:T(8,128)(2,1)S(1)}, bf16[16,80,128]{2,1,0:T(8,128)(2,1)S(1)}, u32[]{:S(2)}, u32[]{:S(2)}) %collective-permute-start) | collective-permute-done | bytes 327712 | tf_op jit(solution)/shard_map/fetch/ppermute | solution.py:439
  35.0 0.0 collective-permute-done.1
  35.0 0.0 collective-permute-done.2
  35.1 2.1 %collective-permute-done.3 = bf16[3,80,128]{2,1,0:T(8,128)(2,1)S(1)} collective-permute-done((bf16[3,80,128]{2,1,0:T(8,128)(2,1)S(1)}, bf16[3,80,128]{2,1,0:T(8,128)(2,1)S(1)}, u32[]{:S(2)}, u32[]{:S(2)}) %collective-permute-start.3) | collective-permute-done | bytes 61472 | tf_op jit(solution)/shard_map/fetch/ppermute | solution.py:439
  37.1 1.3 %collective-permute-start.4 = (bf16[33,80,128]{2,1,0:T(8,128)(2,1)S(1)}, bf16[33,80,128]{2,1,0:T(8,128)(2,1)S(1)}, u32[]{:S(2)}, u32[]{:S(2)}) collective-permute-start(bf16[33,80,128]{2,1,0:T(8,128)(2,1)S(1)} %constant_dynamic-update-slice_fusion.mine_ref), channel_id=1, source_target_pairs={{0,4},{4,0},{8,12},{12,8},{16,20},{20,16},{24,28},{28,24},{32,36},... | collective-permute-start | bytes 2027528 | tf_op jit(solution)/shard_map/fetch/ppermute | solution.py:450
  38.4 1.8 %collective-permute-done.4.theirs_ref = bf16[33,80,128]{2,1,0:T(8,128)(2,1)S(1)} collective-permute-done((bf16[33,80,128]{2,1,0:T(8,128)(2,1)S(1)}, bf16[33,80,128]{2,1,0:T(8,128)(2,1)S(1)}, u32[]{:S(2)}, u32[]{:S(2)}) %collective-permute-start.4) | collective-permute-done | bytes 675872 | tf_op jit(solution)/shard_map/fetch/ppermute | solution.py:450
  40.1 0.0 copy-done.1
  40.1 0.0 copy-done
  40.1 18.8 %joint.1 = (f32[6,1280]{1,0:T(8,128)S(1)}, f32[6,1280]{1,0:T(8,128)S(1)}, f32[24,320]{1,0:T(8,128)S(1)}) custom-call(bf16[24,640]{1,0:T(8,128)(2,1)S(1)} %bitcast.53, bf16[16,80,128]{2,1,0:T(8,128)(2,1)S(1)} %bitcast.51, bf16[6,80,128]{2,1,0:T(8,128)(2,1)S(1)} %copy-done, bf16[33,80,128]{2,1,0:T(8,128)(2,1)S(1)} %constant_dynamic-update-slice_fusion.mine_ref, ...), custom_call_target="tpu_custom_call" | custom-call | flops 10066329600 | bytes 2097152 | tf_op jit(solution)/shard_map/joint/pallas_call | solution.py:193
  59.0 0.1 reshape.23
  59.0 0.1 reshape.22
  59.1 1.2 %collective-permute-start.5 = (f32[3,24,320]{2,1,0:T(8,128)S(1)}, f32[3,24,320]{2,1,0:T(8,128)S(1)}, u32[]{:S(2)}, u32[]{:S(2)}) collective-permute-start(f32[3,24,320]{2,1,0:T(8,128)S(1)} %pad_maximum_fusion), channel_id=1, source_target_pairs={{0,1},{1,2},{2,3},{3,0},{4,5},{5,6},{6,7},{7,4},{8,9},{9,10},{10,1... | collective-permute-start | bytes 276488 | tf_op jit(solution)/shard_map/combine_vocab/ppermute | solution.py:419
  61.7 0.1 reshape.24
  61.8 0.1 reshape.21
  61.8 2.6 %collective-permute-start.6 = (f32[3,24,320]{2,1,0:T(8,128)S(1)}, f32[3,24,320]{2,1,0:T(8,128)S(1)}, u32[]{:S(2)}, u32[]{:S(2)}) collective-permute-start(f32[3,24,320]{2,1,0:T(8,128)S(1)} %pad_maximum_fusion), channel_id=1, source_target_pairs={{0,2},{1,3},{2,0},{3,1},{4,6},{5,7},{6,4},{7,5},{8,10},{9,11},{10,... | collective-permute-start | bytes 276488 | tf_op jit(solution)/shard_map/combine_vocab/ppermute | solution.py:419
  64.5 1.1 %collective-permute-start.7 = (f32[3,24,320]{2,1,0:T(8,128)S(1)}, f32[3,24,320]{2,1,0:T(8,128)S(1)}, u32[]{:S(2)}, u32[]{:S(2)}) collective-permute-start(f32[3,24,320]{2,1,0:T(8,128)S(1)} %pad_maximum_fusion), channel_id=1, source_target_pairs={{0,3},{1,0},{2,1},{3,2},{4,7},{5,4},{6,5},{7,6},{8,11},{9,8},{10,9... | collective-permute-start | bytes 276488 | tf_op jit(solution)/shard_map/combine_vocab/ppermute | solution.py:419
  65.5 0.0 collective-permute-done.5
  65.6 2.8 %collective-permute-done.6 = f32[3,24,320]{2,1,0:T(8,128)S(1)} collective-permute-done((f32[3,24,320]{2,1,0:T(8,128)S(1)}, f32[3,24,320]{2,1,0:T(8,128)S(1)}, u32[]{:S(2)}, u32[]{:S(2)}) %collective-permute-start.6) | collective-permute-done | bytes 92192 | tf_op jit(solution)/shard_map/combine_vocab/ppermute | solution.py:419
  68.4 0.8 collective-permute-done.7
  69.3 19.1 %all-gather.1 = f32[32,24,320]{2,1,0:T(8,128)S(1)} all-gather(f32[2,24,320]{2,1,0:T(8,128)S(1)} %pad_maximum_fusion.1), channel_id=3, replica_groups=mesh['batch'=4,'tm'=16,'label'=4] {'tm'}, dimensions={0}, use_global_device_ids=true | all-gather | bytes 1044480 | tf_op jit(solution)/shard_map/gather_grid/all_gather | solution.py:463
  88.4 8.4 %lattice.1 = (f32[1,1]{1,0:T(1,128)}, f32[24,80]{1,0:T(8,128)}, f32[24,80]{1,0:T(8,128)}) custom-call(s32[1]{0:T(128)S(6)} %copy.12.frame_len_ref, s32[1]{0:T(128)S(6)} %copy.13.label_len_ref, f32[16,2,24,320]{3,2,1,0:T(8,128)S(1)} %bitcast.48), custom_call_target="tpu_custom_call" | custom-call | tf_op jit(solution)/shard_map/lattice/pallas_call | solution.py:398
  (12 shorter events, 0.2 us)
Async XLA Ops:
  0.6 39.5 %copy-start.1 = (bf16[1,24,640]{2,1,0:T(8,128)(2,1)S(1)}, bf16[1,24,640]{2,1,0:T(8,128)(2,1)}, u32[]{:S(2)}) copy-start(bf16[1,24,640]{2,1,0:T(8,128)(2,1)} %param.6) | copy-start | bytes 92164
  2.4 37.8 %copy-start = (bf16[6,80,128]{2,1,0:T(8,128)(2,1)S(1)}, bf16[6,80,128]{2,1,0:T(8,128)(2,1)}, u32[]{:S(2)}) copy-start(bf16[6,80,128]{2,1,0:T(8,128)(2,1)} %get-tuple-element.21.own_pred_ref) | copy-start | bytes 368644
  24.9 10.0 %collective-permute-start = (bf16[16,80,128]{2,1,0:T(8,128)(2,1)S(1)}, bf16[16,80,128]{2,1,0:T(8,128)(2,1)S(1)}, u32[]{:S(2)}, u32[]{:S(2)}) collective-permute-start(bf16[16,80,128]{2,1,0:T(8,128)(2,1)S(1)} %bitcast.49), channel_id=1, source_target_pairs={{0,64},{4,196},{8,72},{12,204},{16,80},{20,212},{24,88},{28,220},{... | collective-permute-start | bytes 983048 | tf_op jit(solution)/shard_map/fetch/ppermute | solution.py:439
  27.4 7.5 %collective-permute-start.1 = (bf16[8,80,128]{2,1,0:T(8,128)(2,1)S(1)}, bf16[8,80,128]{2,1,0:T(8,128)(2,1)S(1)}, u32[]{:S(2)}, u32[]{:S(2)}) collective-permute-start(bf16[8,80,128]{2,1,0:T(8,128)(2,1)S(1)} %constant_dynamic-slice_fusion.1), channel_id=1, source_target_pairs={{0,128},{4,132},{8,136},{12,140},{16,144},{20,148},{24,152},{28,15... | collective-permute-start | bytes 491528 | tf_op jit(solution)/shard_map/fetch/ppermute | solution.py:439
  28.0 7.0 %collective-permute-start.2 = (bf16[6,80,128]{2,1,0:T(8,128)(2,1)}, bf16[6,80,128]{2,1,0:T(8,128)(2,1)S(1)}, u32[]{:S(2)}, u32[]{:S(2)}) collective-permute-start(bf16[6,80,128]{2,1,0:T(8,128)(2,1)} %get-tuple-element.21.own_pred_ref), channel_id=1, source_target_pairs={{0,1},{4,7},{8,9},{12,15},{16,17},{20,23},{24,25},{28,31},{32,33},... | collective-permute-start | bytes 368648 | tf_op jit(solution)/shard_map/fetch/ppermute | solution.py:439
  31.6 5.5 %collective-permute-start.3 = (bf16[3,80,128]{2,1,0:T(8,128)(2,1)S(1)}, bf16[3,80,128]{2,1,0:T(8,128)(2,1)S(1)}, u32[]{:S(2)}, u32[]{:S(2)}) collective-permute-start(bf16[3,80,128]{2,1,0:T(8,128)(2,1)S(1)} %constant_dynamic-slice_fusion), channel_id=1, source_target_pairs={{0,2},{4,6},{8,10},{12,14},{16,18},{20,22},{24,26},{28,30},{32,34}... | collective-permute-start | bytes 184328 | tf_op jit(solution)/shard_map/fetch/ppermute | solution.py:439
  37.1 3.0 %collective-permute-start.4 = (bf16[33,80,128]{2,1,0:T(8,128)(2,1)S(1)}, bf16[33,80,128]{2,1,0:T(8,128)(2,1)S(1)}, u32[]{:S(2)}, u32[]{:S(2)}) collective-permute-start(bf16[33,80,128]{2,1,0:T(8,128)(2,1)S(1)} %constant_dynamic-update-slice_fusion.mine_ref), channel_id=1, source_target_pairs={{0,4},{4,0},{8,12},{12,8},{16,20},{20,16},{24,28},{28,24},{32,36},... | collective-permute-start | bytes 2027528 | tf_op jit(solution)/shard_map/fetch/ppermute | solution.py:450
  59.1 6.4 %collective-permute-start.5 = (f32[3,24,320]{2,1,0:T(8,128)S(1)}, f32[3,24,320]{2,1,0:T(8,128)S(1)}, u32[]{:S(2)}, u32[]{:S(2)}) collective-permute-start(f32[3,24,320]{2,1,0:T(8,128)S(1)} %pad_maximum_fusion), channel_id=1, source_target_pairs={{0,1},{1,2},{2,3},{3,0},{4,5},{5,6},{6,7},{7,4},{8,9},{9,10},{10,1... | collective-permute-start | bytes 276488 | tf_op jit(solution)/shard_map/combine_vocab/ppermute | solution.py:419
  61.8 6.5 %collective-permute-start.6 = (f32[3,24,320]{2,1,0:T(8,128)S(1)}, f32[3,24,320]{2,1,0:T(8,128)S(1)}, u32[]{:S(2)}, u32[]{:S(2)}) collective-permute-start(f32[3,24,320]{2,1,0:T(8,128)S(1)} %pad_maximum_fusion), channel_id=1, source_target_pairs={{0,2},{1,3},{2,0},{3,1},{4,6},{5,7},{6,4},{7,5},{8,10},{9,11},{10,... | collective-permute-start | bytes 276488 | tf_op jit(solution)/shard_map/combine_vocab/ppermute | solution.py:419
  64.5 4.8 %collective-permute-start.7 = (f32[3,24,320]{2,1,0:T(8,128)S(1)}, f32[3,24,320]{2,1,0:T(8,128)S(1)}, u32[]{:S(2)}, u32[]{:S(2)}) collective-permute-start(f32[3,24,320]{2,1,0:T(8,128)S(1)} %pad_maximum_fusion), channel_id=1, source_target_pairs={{0,3},{1,0},{2,1},{3,2},{4,7},{5,4},{6,5},{7,6},{8,11},{9,8},{10,9... | collective-permute-start | bytes 276488 | tf_op jit(solution)/shard_map/combine_vocab/ppermute | solution.py:419

commit v3 on v2

--- a/solution.py
+++ b/solution.py
@@ -453,11 +453,12 @@
         blank = jnp.where(mine == 0, blank, 0.0)
         parts = jnp.stack([lse.reshape(picked.shape), blank.reshape(picked.shape), picked])
         parts = around(parts, "label")
-        norm, log_blank, log_label = parts[0]
-        for part in parts[1:]:
-            norm = jnp.logaddexp(norm, part[0])
-            log_blank, log_label = log_blank + part[1], log_label + part[2]
-            norm, log_blank, log_label = lax.optimization_barrier((norm, log_blank, log_label))
+
+        def merge_parts(one, two):
+            return jnp.logaddexp(one[0], two[0]), one[1] + two[1], one[2] + two[2]
+
+        here = lax.optimization_barrier(merge_parts(parts[0], parts[2]))
+        norm, log_blank, log_label = merge_parts(here, merge_parts(parts[1], parts[3]))
         log_blank, log_label = log_blank - norm, log_label - norm
     with jax.named_scope("gather_grid"):
         grid = lax.all_gather(jnp.stack([log_blank, log_label]), "tm", axis=0, tiled=False)

time: 97 us -> 96.6 us (level)
  waiting for transfers between devices: 10.4 us -> 9.19 us
    ppermute x3, waiting for transfers between devices: 3.61 us -> 2.42 us  [around(): lax.ppermute(array, axis, [(i, (i + by) % size) for i in range(size)])]
  transfers between devices with their start and end apart: 8 -> 8, of which waited for: 5 -> 4; matrix products, arithmetic and copies ran while one was open for 1% -> 1% of each run, Pallas kernels for 0% -> 0%
where the time goes in v3:
time: 96.6 us; the launch traced here: 96.4 us
  blocking collectives  41.9 us (43%)
  Pallas kernels  28.9 us (30%)
  starting transfers between devices  13 us (13%)
  waiting for transfers between devices  9.19 us (10%)
  between operations  2.01 us (2%)
  local copies, waits for them, and re-layouts  1.29 us (1%)
    all_gather x1, blocking collectives, shards(): own = lax.all_gather(own, 'tm', axis=0, tiled=False)  22.6 us
    all_gather x1, blocking collectives, shards(): lax.all_gather(jnp.stack([log_blank, log_label]), 'tm', axis=0, tiled=False)  19.4 us
    pallas_call x1, Pallas kernels, joint_terms(): pl.pallas_call(joint_kernel, out_shape=(grouped, grouped, jax.ShapeDtypeS...  18.8 us
    pallas_call x1, Pallas kernels, lattice_loss(): pl.pallas_call(lattice_kernel, out_shape=(jax.ShapeDtypeStruct((1, 1), F3...  8.36 us
    ppermute x4, starting transfers between devices, both_ways(): return (lax.ppermute(array, axes, near), lax.ppermute(half, axes, opposite))  6.17 us
    ppermute x3, starting transfers between devices, around(): lax.ppermute(array, axis, [(i, (i + by) % size) for i in range(size)])  5.55 us
    ppermute x4, waiting for transfers between devices, both_ways(): return (lax.ppermute(array, axes, near), lax.ppermute(half, axes, opposite))  5.01 us
    ppermute x3, waiting for transfers between devices, around(): lax.ppermute(array, axis, [(i, (i + by) % size) for i in range(size)])  2.42 us
  transfers between devices with their start and end apart: 8, of which 4 were waited for; matrix products, arithmetic and copies ran while one was open for 1% of the time, Pallas kernels for 0%

profile of v3, /device:TPU:1, one launch (start us, length us, event | category | flops | bytes accessed | tf_op | source)
XLA Modules:
  0.0 96.4 jit_solution(7852710066556297425)
XLA Ops:
  0.6 0.0 copy-start.1
  0.6 1.7 %pack.1 = (bf16[80,128]{1,0:T(8,128)(2,1)}, bf16[6,80,128]{2,1,0:T(8,128)(2,1)}) custom-call(bf16[160,256]{1,0:T(8,128)(2,1)} %weight_ref.1, bf16[80,640]{1,0:T(8,128)(2,1)} %bitcast.62, s32[1,80]{1,0:T(1,128)} %labels_ref.1), custom_call_target="tpu_custom_call" | custom-call | tf_op jit(solution)/shard_map/pack/pallas_call | solution.py:48
  2.4 0.0 copy-start
  2.4 22.6 %all-gather = bf16[1280,128]{1,0:T(8,128)(2,1)S(1)} all-gather(bf16[80,128]{1,0:T(8,128)(2,1)} %get-tuple-element.14), channel_id=2, replica_groups=mesh['batch'=4,'tm'=16,'label'=4] {'tm'}, dimensions={0}, use_global_device_ids=true | all-gather | bytes 348160 | tf_op jit(solution)/shard_map/gather_weight/all_gather | solution.py:446
  24.9 2.5 %collective-permute-start = (bf16[16,80,128]{2,1,0:T(8,128)(2,1)S(1)}, bf16[16,80,128]{2,1,0:T(8,128)(2,1)S(1)}, u32[]{:S(2)}, u32[]{:S(2)}) collective-permute-start(bf16[16,80,128]{2,1,0:T(8,128)(2,1)S(1)} %bitcast.57), channel_id=1, source_target_pairs={{0,64},{4,196},{8,72},{12,204},{16,80},{20,212},{24,88},{28,220},{... | collective-permute-start | bytes 983048 | tf_op jit(solution)/shard_map/fetch/ppermute | solution.py:439
  27.4 0.6 collective-permute-start.1
  28.0 2.7 %collective-permute-start.2 = (bf16[6,80,128]{2,1,0:T(8,128)(2,1)}, bf16[6,80,128]{2,1,0:T(8,128)(2,1)S(1)}, u32[]{:S(2)}, u32[]{:S(2)}) collective-permute-start(bf16[6,80,128]{2,1,0:T(8,128)(2,1)} %get-tuple-element.15.own_pred_ref), channel_id=1, source_target_pairs={{0,1},{4,7},{8,9},{12,15},{16,17},{20,23},{24,25},{28,31},{32,33},... | collective-permute-start | bytes 368648 | tf_op jit(solution)/shard_map/fetch/ppermute | solution.py:439
  30.8 0.9 constant_dynamic-slice_fusion
  31.6 0.3 collective-permute-start.3
  32.0 3.0 %collective-permute-done = bf16[16,80,128]{2,1,0:T(8,128)(2,1)S(1)} collective-permute-done((bf16[16,80,128]{2,1,0:T(8,128)(2,1)S(1)}, bf16[16,80,128]{2,1,0:T(8,128)(2,1)S(1)}, u32[]{:S(2)}, u32[]{:S(2)}) %collective-permute-start) | collective-permute-done | bytes 327712 | tf_op jit(solution)/shard_map/fetch/ppermute | solution.py:439
  35.0 0.0 collective-permute-done.1
  35.0 0.0 collective-permute-done.2
  35.1 2.1 %collective-permute-done.3 = bf16[3,80,128]{2,1,0:T(8,128)(2,1)S(1)} collective-permute-done((bf16[3,80,128]{2,1,0:T(8,128)(2,1)S(1)}, bf16[3,80,128]{2,1,0:T(8,128)(2,1)S(1)}, u32[]{:S(2)}, u32[]{:S(2)}) %collective-permute-start.3) | collective-permute-done | bytes 61472 | tf_op jit(solution)/shard_map/fetch/ppermute | solution.py:439
  37.1 1.3 %collective-permute-start.4 = (bf16[33,80,128]{2,1,0:T(8,128)(2,1)S(1)}, bf16[33,80,128]{2,1,0:T(8,128)(2,1)S(1)}, u32[]{:S(2)}, u32[]{:S(2)}) collective-permute-start(bf16[33,80,128]{2,1,0:T(8,128)(2,1)S(1)} %constant_dynamic-update-slice_fusion.mine_ref), channel_id=1, source_target_pairs={{0,4},{4,0},{8,12},{12,8},{16,20},{20,16},{24,28},{28,24},{32,36},... | collective-permute-start | bytes 2027528 | tf_op jit(solution)/shard_map/fetch/ppermute | solution.py:450
  38.4 1.8 %collective-permute-done.4.theirs_ref = bf16[33,80,128]{2,1,0:T(8,128)(2,1)S(1)} collective-permute-done((bf16[33,80,128]{2,1,0:T(8,128)(2,1)S(1)}, bf16[33,80,128]{2,1,0:T(8,128)(2,1)S(1)}, u32[]{:S(2)}, u32[]{:S(2)}) %collective-permute-start.4) | collective-permute-done | bytes 675872 | tf_op jit(solution)/shard_map/fetch/ppermute | solution.py:450
  40.1 0.0 copy-done.1
  40.1 0.0 copy-done
  40.2 18.8 %joint.1 = (f32[6,1280]{1,0:T(8,128)S(1)}, f32[6,1280]{1,0:T(8,128)S(1)}, f32[24,320]{1,0:T(8,128)S(1)}) custom-call(bf16[24,640]{1,0:T(8,128)(2,1)S(1)} %bitcast.61, bf16[16,80,128]{2,1,0:T(8,128)(2,1)S(1)} %bitcast.59, bf16[6,80,128]{2,1,0:T(8,128)(2,1)S(1)} %copy-done, bf16[33,80,128]{2,1,0:T(8,128)(2,1)S(1)} %constant_dynamic-update-slice_fusion.mine_ref, ...), custom_call_target="tpu_custom_call" | custom-call | flops 10066329600 | bytes 2097152 | tf_op jit(solution)/shard_map/joint/pallas_call | solution.py:193
  59.0 0.1 reshape.32
  59.1 0.1 reshape.31
  59.2 2.7 %collective-permute-start.5 = (f32[3,24,320]{2,1,0:T(8,128)S(1)}, f32[3,24,320]{2,1,0:T(8,128)S(1)}, u32[]{:S(2)}, u32[]{:S(2)}) collective-permute-start(f32[3,24,320]{2,1,0:T(8,128)S(1)} %pad_maximum_fusion), channel_id=1, source_target_pairs={{0,2},{1,3},{2,0},{3,1},{4,6},{5,7},{6,4},{7,5},{8,10},{9,11},{10,... | collective-permute-start | bytes 276488 | tf_op jit(solution)/shard_map/combine_vocab/ppermute | solution.py:419
  63.1 0.1 reshape.33
  63.2 0.1 reshape.30
  63.3 0.6 collective-permute-start.6
  63.9 2.3 %collective-permute-start.7 = (f32[3,24,320]{2,1,0:T(8,128)S(1)}, f32[3,24,320]{2,1,0:T(8,128)S(1)}, u32[]{:S(2)}, u32[]{:S(2)}) collective-permute-start(f32[3,24,320]{2,1,0:T(8,128)S(1)} %pad_maximum_fusion), channel_id=1, source_target_pairs={{0,3},{1,0},{2,1},{3,2},{4,7},{5,4},{6,5},{7,6},{8,11},{9,8},{10,9... | collective-permute-start | bytes 276488 | tf_op jit(solution)/shard_map/combine_vocab/ppermute | solution.py:419
  66.2 0.0 collective-permute-done.5
  66.2 2.4 %collective-permute-done.6 = f32[3,24,320]{2,1,0:T(8,128)S(1)} collective-permute-done((f32[3,24,320]{2,1,0:T(8,128)S(1)}, f32[3,24,320]{2,1,0:T(8,128)S(1)}, u32[]{:S(2)}, u32[]{:S(2)}) %collective-permute-start.6) | collective-permute-done | bytes 92192 | tf_op jit(solution)/shard_map/combine_vocab/ppermute | solution.py:419
  68.6 0.0 collective-permute-done.7
  68.6 0.1 fusion.7
  68.7 19.4 %all-gather.1 = f32[32,24,320]{2,1,0:T(8,128)S(1)} all-gather(f32[2,24,320]{2,1,0:T(8,128)S(1)} %pad_maximum_fusion.1), channel_id=3, replica_groups=mesh['batch'=4,'tm'=16,'label'=4] {'tm'}, dimensions={0}, use_global_device_ids=true | all-gather | bytes 1044480 | tf_op jit(solution)/shard_map/gather_grid/all_gather | solution.py:464
  88.1 8.4 %lattice.1 = (f32[1,1]{1,0:T(1,128)}, f32[24,80]{1,0:T(8,128)}, f32[24,80]{1,0:T(8,128)}) custom-call(s32[1]{0:T(128)S(6)} %copy.12.frame_len_ref, s32[1]{0:T(128)S(6)} %copy.13.label_len_ref, f32[16,2,24,320]{3,2,1,0:T(8,128)S(1)} %bitcast.56), custom_call_target="tpu_custom_call" | custom-call | tf_op jit(solution)/shard_map/lattice/pallas_call | solution.py:398
  (9 shorter events, 0.2 us)
Async XLA Ops:
  0.6 39.5 %copy-start.1 = (bf16[1,24,640]{2,1,0:T(8,128)(2,1)S(1)}, bf16[1,24,640]{2,1,0:T(8,128)(2,1)}, u32[]{:S(2)}) copy-start(bf16[1,24,640]{2,1,0:T(8,128)(2,1)} %param.6) | copy-start | bytes 92164
  2.4 37.8 %copy-start = (bf16[6,80,128]{2,1,0:T(8,128)(2,1)S(1)}, bf16[6,80,128]{2,1,0:T(8,128)(2,1)}, u32[]{:S(2)}) copy-start(bf16[6,80,128]{2,1,0:T(8,128)(2,1)} %get-tuple-element.15.own_pred_ref) | copy-start | bytes 368644
  24.9 10.0 %collective-permute-start = (bf16[16,80,128]{2,1,0:T(8,128)(2,1)S(1)}, bf16[16,80,128]{2,1,0:T(8,128)(2,1)S(1)}, u32[]{:S(2)}, u32[]{:S(2)}) collective-permute-start(bf16[16,80,128]{2,1,0:T(8,128)(2,1)S(1)} %bitcast.57), channel_id=1, source_target_pairs={{0,64},{4,196},{8,72},{12,204},{16,80},{20,212},{24,88},{28,220},{... | collective-permute-start | bytes 983048 | tf_op jit(solution)/shard_map/fetch/ppermute | solution.py:439
  27.4 7.5 %collective-permute-start.1 = (bf16[8,80,128]{2,1,0:T(8,128)(2,1)S(1)}, bf16[8,80,128]{2,1,0:T(8,128)(2,1)S(1)}, u32[]{:S(2)}, u32[]{:S(2)}) collective-permute-start(bf16[8,80,128]{2,1,0:T(8,128)(2,1)S(1)} %constant_dynamic-slice_fusion.1), channel_id=1, source_target_pairs={{0,128},{4,132},{8,136},{12,140},{16,144},{20,148},{24,152},{28,15... | collective-permute-start | bytes 491528 | tf_op jit(solution)/shard_map/fetch/ppermute | solution.py:439
  28.0 7.0 %collective-permute-start.2 = (bf16[6,80,128]{2,1,0:T(8,128)(2,1)}, bf16[6,80,128]{2,1,0:T(8,128)(2,1)S(1)}, u32[]{:S(2)}, u32[]{:S(2)}) collective-permute-start(bf16[6,80,128]{2,1,0:T(8,128)(2,1)} %get-tuple-element.15.own_pred_ref), channel_id=1, source_target_pairs={{0,1},{4,7},{8,9},{12,15},{16,17},{20,23},{24,25},{28,31},{32,33},... | collective-permute-start | bytes 368648 | tf_op jit(solution)/shard_map/fetch/ppermute | solution.py:439
  31.6 5.5 %collective-permute-start.3 = (bf16[3,80,128]{2,1,0:T(8,128)(2,1)S(1)}, bf16[3,80,128]{2,1,0:T(8,128)(2,1)S(1)}, u32[]{:S(2)}, u32[]{:S(2)}) collective-permute-start(bf16[3,80,128]{2,1,0:T(8,128)(2,1)S(1)} %constant_dynamic-slice_fusion), channel_id=1, source_target_pairs={{0,2},{4,6},{8,10},{12,14},{16,18},{20,22},{24,26},{28,30},{32,34}... | collective-permute-start | bytes 184328 | tf_op jit(solution)/shard_map/fetch/ppermute | solution.py:439
  37.1 3.0 %collective-permute-start.4 = (bf16[33,80,128]{2,1,0:T(8,128)(2,1)S(1)}, bf16[33,80,128]{2,1,0:T(8,128)(2,1)S(1)}, u32[]{:S(2)}, u32[]{:S(2)}) collective-permute-start(bf16[33,80,128]{2,1,0:T(8,128)(2,1)S(1)} %constant_dynamic-update-slice_fusion.mine_ref), channel_id=1, source_target_pairs={{0,4},{4,0},{8,12},{12,8},{16,20},{20,16},{24,28},{28,24},{32,36},... | collective-permute-start | bytes 2027528 | tf_op jit(solution)/shard_map/fetch/ppermute | solution.py:450
  59.2 7.0 %collective-permute-start.5 = (f32[3,24,320]{2,1,0:T(8,128)S(1)}, f32[3,24,320]{2,1,0:T(8,128)S(1)}, u32[]{:S(2)}, u32[]{:S(2)}) collective-permute-start(f32[3,24,320]{2,1,0:T(8,128)S(1)} %pad_maximum_fusion), channel_id=1, source_target_pairs={{0,2},{1,3},{2,0},{3,1},{4,6},{5,7},{6,4},{7,5},{8,10},{9,11},{10,... | collective-permute-start | bytes 276488 | tf_op jit(solution)/shard_map/combine_vocab/ppermute | solution.py:419
  63.3 5.3 %collective-permute-start.6 = (f32[3,24,320]{2,1,0:T(8,128)S(1)}, f32[3,24,320]{2,1,0:T(8,128)S(1)}, u32[]{:S(2)}, u32[]{:S(2)}) collective-permute-start(f32[3,24,320]{2,1,0:T(8,128)S(1)} %pad_maximum_fusion), channel_id=1, source_target_pairs={{0,1},{1,2},{2,3},{3,0},{4,5},{5,6},{6,7},{7,4},{8,9},{9,10},{10,1... | collective-permute-start | bytes 276488 | tf_op jit(solution)/shard_map/combine_vocab/ppermute | solution.py:419
  63.9 4.7 %collective-permute-start.7 = (f32[3,24,320]{2,1,0:T(8,128)S(1)}, f32[3,24,320]{2,1,0:T(8,128)S(1)}, u32[]{:S(2)}, u32[]{:S(2)}) collective-permute-start(f32[3,24,320]{2,1,0:T(8,128)S(1)} %pad_maximum_fusion), channel_id=1, source_target_pairs={{0,3},{1,0},{2,1},{3,2},{4,7},{5,4},{6,5},{7,6},{8,11},{9,8},{10,9... | collective-permute-start | bytes 276488 | tf_op jit(solution)/shard_map/combine_vocab/ppermute | solution.py:419

commit v4 on v3

--- a/solution.py
+++ b/solution.py
@@ -58,7 +58,7 @@
 
 
 def joint_kernel(
-    enc_ref, own_ref, own_pred_ref, mine_ref, theirs_ref,
+    enc_ref, own_ref, own_pred_ref, near_mine_ref, mine_ref, near_theirs_ref, theirs_ref,
     lse_ref, blank_ref, picked_ref,
     enc, pred, chosen, picks, columns_first, weight, hidden_a, hidden_b, logits_a, logits_b, top, total, top_a, top_b,
 ):
@@ -90,12 +90,12 @@
 
     put_rows(own_ref, 0, blocks, batch, 0)
     put_positions(own_pred_ref, 0, tiles, mine, 0)
-    for ref, side in ((mine_ref, core), (theirs_ref, 1 - core)):
+    for near, ref, side in ((near_mine_ref, mine_ref, core), (near_theirs_ref, theirs_ref, 1 - core)):
         step = 2 * side - 1
-        put_rows(ref, 0, blocks, wrap(batch + step, BATCH_WAYS), 0)
-        put_rows(ref, blocks, some, wrap(batch + 2, BATCH_WAYS), side * (some // 2))
-        put_positions(ref, blocks + some, tiles, wrap(mine + step, LABEL_WAYS), 0)
-        put_positions(ref, blocks + some + tiles, tiles // 2, wrap(mine + 2, LABEL_WAYS), side * (tiles // 2))
+        put_rows(near, 0, blocks, wrap(batch + step, BATCH_WAYS), 0)
+        put_rows(ref, 0, some, wrap(batch + 2, BATCH_WAYS), side * (some // 2))
+        put_positions(ref, some, tiles, wrap(mine + step, LABEL_WAYS), 0)
+        put_positions(ref, some + tiles, tiles // 2, wrap(mine + 2, LABEL_WAYS), side * (tiles // 2))
     depth = lax.broadcasted_iota(jnp.int32, (128, width), 1)
     upper = lax.rem(depth, 2 * half_rows) < half_rows
     for tile in range(share // 128):
@@ -180,7 +180,7 @@
     picked_ref[...] = picks[...].T[:frames, :]
 
 
-def joint_terms(enc, own, own_pred, mine, theirs):
+def joint_terms(enc, own, own_pred, near_mine, mine, near_theirs, theirs):
     frames, width = enc.shape
     tiles = own_pred.shape[0]
     positions = LABEL_WAYS * own_pred.shape[1]
@@ -193,7 +193,7 @@
     return pl.pallas_call(
         joint_kernel,
         out_shape=(grouped, grouped, jax.ShapeDtypeStruct((frames, positions), F32)),
-        in_specs=[vmem] * 5,
+        in_specs=[vmem] * 7,
         out_specs=(vmem,) * 3,
         scratch_shapes=[
             pltpu.VMEM((frames, width), F32),
@@ -214,7 +214,7 @@
         compiler_params=pltpu.CompilerParams(vmem_limit_bytes=48 << 20),
         cost_estimate=pl.CostEstimate(flops=flops, bytes_accessed=2 << 20, transcendentals=0),
         name="joint",
-    )(enc, own, own_pred, mine, theirs)
+    )(enc, own, own_pred, near_mine, mine, near_theirs, theirs)
 
 
 def tree(combine, terms):
@@ -445,10 +445,12 @@
     with jax.named_scope("gather_weight"):
         own = lax.all_gather(own, "tm", axis=0, tiled=False)
     with jax.named_scope("fetch"):
-        from_others = jnp.concatenate([*both_ways(own, "batch"), *both_ways(own_pred, "label")], axis=0)
+        near, opposite = both_ways(own, "batch")
+        rest = jnp.concatenate([opposite, *both_ways(own_pred, "label")], axis=0)
         swap = [(i, i ^ 1) for i in range(lax.axis_size("tm"))]
-        theirs = lax.ppermute(from_others, "tm", swap)
-    lse, blank, picked = joint_terms(enc_joint[0], own, own_pred, from_others, theirs)
+        near_theirs = lax.ppermute(near, "tm", swap)
+        theirs = lax.ppermute(rest, "tm", swap)
+    lse, blank, picked = joint_terms(enc_joint[0], own, own_pred, near, rest, near_theirs, theirs)
     with jax.named_scope("combine_vocab"):
         blank = jnp.where(mine == 0, blank, 0.0)
         parts = jnp.stack([lse.reshape(picked.shape), blank.reshape(picked.shape), picked])

time: 96.6 us -> 95.4 us (0.988)
  transfers between devices with their start and end apart: 8 -> 9, of which waited for: 4 -> 5; matrix products, arithmetic and copies ran while one was open for 1% -> 1% of each run, Pallas kernels for 0% -> 0%
where the time goes in v4:
time: 95.4 us; the launch traced here: 95.2 us
  blocking collectives  41.9 us (44%)
  Pallas kernels  28.9 us (30%)
  starting transfers between devices  12.6 us (13%)
  waiting for transfers between devices  8.42 us (9%)
  between operations  2.01 us (2%)
  local copies, waits for them, and re-layouts  1.25 us (1%)
    all_gather x1, blocking collectives, shards(): own = lax.all_gather(own, 'tm', axis=0, tiled=False)  22.6 us
    all_gather x1, blocking collectives, shards(): lax.all_gather(jnp.stack([log_blank, log_label]), 'tm', axis=0, tiled=False)  19.3 us
    pallas_call x1, Pallas kernels, joint_terms(): pl.pallas_call(joint_kernel, out_shape=(grouped, grouped, jax.ShapeDtypeS...  18.8 us
    pallas_call x1, Pallas kernels, lattice_loss(): pl.pallas_call(lattice_kernel, out_shape=(jax.ShapeDtypeStruct((1, 1), F3...  8.36 us
    ppermute x4, starting transfers between devices, both_ways(): return (lax.ppermute(array, axes, near), lax.ppermute(half, axes, opposite))  6.77 us
    ppermute x3, starting transfers between devices, around(): lax.ppermute(array, axis, [(i, (i + by) % size) for i in range(size)])  5.21 us
    ppermute x4, waiting for transfers between devices, both_ways(): return (lax.ppermute(array, axes, near), lax.ppermute(half, axes, opposite))  4.36 us
    ppermute x3, waiting for transfers between devices, around(): lax.ppermute(array, axis, [(i, (i + by) % size) for i in range(size)])  2.45 us
  transfers between devices with their start and end apart: 9, of which 5 were waited for; matrix products, arithmetic and copies ran while one was open for 1% of the time, Pallas kernels for 0%

profile of v4, /device:TPU:1, one launch (start us, length us, event | category | flops | bytes accessed | tf_op | source)
XLA Modules:
  0.0 95.2 jit_solution(2447984329035578489)
XLA Ops:
  0.6 0.0 copy-start.1
  0.7 1.7 %pack.1 = (bf16[80,128]{1,0:T(8,128)(2,1)}, bf16[6,80,128]{2,1,0:T(8,128)(2,1)}) custom-call(bf16[160,256]{1,0:T(8,128)(2,1)} %weight_ref.1, bf16[80,640]{1,0:T(8,128)(2,1)} %bitcast.62, s32[1,80]{1,0:T(1,128)} %labels_ref.1), custom_call_target="tpu_custom_call" | custom-call | tf_op jit(solution)/shard_map/pack/pallas_call | solution.py:48
  2.4 0.0 copy-start
  2.4 22.6 %all-gather = bf16[1280,128]{1,0:T(8,128)(2,1)S(1)} all-gather(bf16[80,128]{1,0:T(8,128)(2,1)} %get-tuple-element.14), channel_id=2, replica_groups=mesh['batch'=4,'tm'=16,'label'=4] {'tm'}, dimensions={0}, use_global_device_ids=true | all-gather | bytes 348160 | tf_op jit(solution)/shard_map/gather_weight/all_gather | solution.py:446
  25.0 2.8 %collective-permute-start.1 = (bf16[8,80,128]{2,1,0:T(8,128)(2,1)S(1)}, bf16[8,80,128]{2,1,0:T(8,128)(2,1)S(1)}, u32[]{:S(2)}, u32[]{:S(2)}) collective-permute-start(bf16[8,80,128]{2,1,0:T(8,128)(2,1)S(1)} %constant_dynamic-slice_fusion.1), channel_id=1, source_target_pairs={{0,128},{4,132},{8,136},{12,140},{16,144},{20,148},{24,152},{28,15... | collective-permute-start | bytes 491528 | tf_op jit(solution)/shard_map/fetch/ppermute | solution.py:439
  27.8 0.9 collective-permute-start
  28.7 2.7 %collective-permute-start.2 = (bf16[6,80,128]{2,1,0:T(8,128)(2,1)}, bf16[6,80,128]{2,1,0:T(8,128)(2,1)S(1)}, u32[]{:S(2)}, u32[]{:S(2)}) collective-permute-start(bf16[6,80,128]{2,1,0:T(8,128)(2,1)} %get-tuple-element.15.own_pred_ref), channel_id=1, source_target_pairs={{0,1},{4,7},{8,9},{12,15},{16,17},{20,23},{24,25},{28,31},{32,33},... | collective-permute-start | bytes 368648 | tf_op jit(solution)/shard_map/fetch/ppermute | solution.py:439
  31.4 0.9 constant_dynamic-slice_fusion
  32.3 0.3 collective-permute-start.3
  32.6 0.0 collective-permute-done.1
  32.6 1.0 collective-permute-done.2
  33.6 3.4 %collective-permute-done.3 = bf16[3,80,128]{2,1,0:T(8,128)(2,1)S(1)} collective-permute-done((bf16[3,80,128]{2,1,0:T(8,128)(2,1)S(1)}, bf16[3,80,128]{2,1,0:T(8,128)(2,1)S(1)}, u32[]{:S(2)}, u32[]{:S(2)}) %collective-permute-start.3) | collective-permute-done | bytes 61472 | tf_op jit(solution)/shard_map/fetch/ppermute | solution.py:439
  37.0 0.2 collective-permute-start.5
  37.2 0.0 collective-permute-done.near_mine_ref
  37.2 0.4 collective-permute-start.4
  37.6 1.1 %collective-permute-done.5.theirs_ref = bf16[17,80,128]{2,1,0:T(8,128)(2,1)S(1)} collective-permute-done((bf16[17,80,128]{2,1,0:T(8,128)(2,1)S(1)}, bf16[17,80,128]{2,1,0:T(8,128)(2,1)S(1)}, u32[]{:S(2)}, u32[]{:S(2)}) %collective-permute-start.5) | collective-permute-done | bytes 348192 | tf_op jit(solution)/shard_map/fetch/ppermute | solution.py:452
  38.8 0.5 collective-permute-done.4.near_theirs_ref
  39.2 0.0 copy-done.1
  39.2 0.0 copy-done
  39.2 18.8 %joint.1 = (f32[6,1280]{1,0:T(8,128)S(1)}, f32[6,1280]{1,0:T(8,128)S(1)}, f32[24,320]{1,0:T(8,128)S(1)}) custom-call(bf16[24,640]{1,0:T(8,128)(2,1)S(1)} %bitcast.61, bf16[16,80,128]{2,1,0:T(8,128)(2,1)S(1)} %bitcast.59, bf16[6,80,128]{2,1,0:T(8,128)(2,1)S(1)} %copy-done, bf16[16,80,128]{2,1,0:T(8,128)(2,1)S(1)} %collective-permute-done.near_mine_ref, ...), custom_call_target="tpu_custom_call" | custom-call | flops 10066329600 | bytes 2097152 | tf_op jit(solution)/shard_map/joint/pallas_call | solution.py:193
  58.1 0.1 reshape.32
  58.1 0.1 reshape.31
  58.2 2.5 %collective-permute-start.6 = (f32[3,24,320]{2,1,0:T(8,128)S(1)}, f32[3,24,320]{2,1,0:T(8,128)S(1)}, u32[]{:S(2)}, u32[]{:S(2)}) collective-permute-start(f32[3,24,320]{2,1,0:T(8,128)S(1)} %pad_maximum_fusion), channel_id=1, source_target_pairs={{0,2},{1,3},{2,0},{3,1},{4,6},{5,7},{6,4},{7,5},{8,10},{9,11},{10,... | collective-permute-start | bytes 276488 | tf_op jit(solution)/shard_map/combine_vocab/ppermute | solution.py:419
  62.1 0.1 reshape.33
  62.1 0.1 reshape.30
  62.2 0.0 collective-permute-start.7
  62.2 2.7 %collective-permute-start.8 = (f32[3,24,320]{2,1,0:T(8,128)S(1)}, f32[3,24,320]{2,1,0:T(8,128)S(1)}, u32[]{:S(2)}, u32[]{:S(2)}) collective-permute-start(f32[3,24,320]{2,1,0:T(8,128)S(1)} %pad_maximum_fusion), channel_id=1, source_target_pairs={{0,3},{1,0},{2,1},{3,2},{4,7},{5,4},{6,5},{7,6},{8,11},{9,8},{10,9... | collective-permute-start | bytes 276488 | tf_op jit(solution)/shard_map/combine_vocab/ppermute | solution.py:419
  64.9 0.0 collective-permute-done.6
  65.0 2.4 %collective-permute-done.7 = f32[3,24,320]{2,1,0:T(8,128)S(1)} collective-permute-done((f32[3,24,320]{2,1,0:T(8,128)S(1)}, f32[3,24,320]{2,1,0:T(8,128)S(1)}, u32[]{:S(2)}, u32[]{:S(2)}) %collective-permute-start.7) | collective-permute-done | bytes 92192 | tf_op jit(solution)/shard_map/combine_vocab/ppermute | solution.py:419
  67.4 0.0 collective-permute-done.8
  67.4 0.1 fusion.7
  67.5 19.3 %all-gather.1 = f32[32,24,320]{2,1,0:T(8,128)S(1)} all-gather(f32[2,24,320]{2,1,0:T(8,128)S(1)} %pad_maximum_fusion.1), channel_id=3, replica_groups=mesh['batch'=4,'tm'=16,'label'=4] {'tm'}, dimensions={0}, use_global_device_ids=true | all-gather | bytes 1044480 | tf_op jit(solution)/shard_map/gather_grid/all_gather | solution.py:466
  86.8 8.4 %lattice.1 = (f32[1,1]{1,0:T(1,128)}, f32[24,80]{1,0:T(8,128)}, f32[24,80]{1,0:T(8,128)}) custom-call(s32[1]{0:T(128)S(6)} %copy.11.frame_len_ref, s32[1]{0:T(128)S(6)} %copy.12.label_len_ref, f32[16,2,24,320]{3,2,1,0:T(8,128)S(1)} %bitcast.56), custom_call_target="tpu_custom_call" | custom-call | tf_op jit(solution)/shard_map/lattice/pallas_call | solution.py:398
  (8 shorter events, 0.1 us)
Async XLA Ops:
  0.6 38.6 %copy-start.1 = (bf16[1,24,640]{2,1,0:T(8,128)(2,1)S(1)}, bf16[1,24,640]{2,1,0:T(8,128)(2,1)}, u32[]{:S(2)}) copy-start(bf16[1,24,640]{2,1,0:T(8,128)(2,1)} %param.6) | copy-start | bytes 92164
  2.4 36.9 %copy-start = (bf16[6,80,128]{2,1,0:T(8,128)(2,1)S(1)}, bf16[6,80,128]{2,1,0:T(8,128)(2,1)}, u32[]{:S(2)}) copy-start(bf16[6,80,128]{2,1,0:T(8,128)(2,1)} %get-tuple-element.15.own_pred_ref) | copy-start | bytes 368644
  25.0 7.6 %collective-permute-start.1 = (bf16[8,80,128]{2,1,0:T(8,128)(2,1)S(1)}, bf16[8,80,128]{2,1,0:T(8,128)(2,1)S(1)}, u32[]{:S(2)}, u32[]{:S(2)}) collective-permute-start(bf16[8,80,128]{2,1,0:T(8,128)(2,1)S(1)} %constant_dynamic-slice_fusion.1), channel_id=1, source_target_pairs={{0,128},{4,132},{8,136},{12,140},{16,144},{20,148},{24,152},{28,15... | collective-permute-start | bytes 491528 | tf_op jit(solution)/shard_map/fetch/ppermute | solution.py:439
  27.8 9.4 %collective-permute-start = (bf16[16,80,128]{2,1,0:T(8,128)(2,1)S(1)}, bf16[16,80,128]{2,1,0:T(8,128)(2,1)S(1)}, u32[]{:S(2)}, u32[]{:S(2)}) collective-permute-start(bf16[16,80,128]{2,1,0:T(8,128)(2,1)S(1)} %bitcast.58), channel_id=1, source_target_pairs={{0,64},{4,196},{8,72},{12,204},{16,80},{20,212},{24,88},{28,220},{... | collective-permute-start | bytes 983048 | tf_op jit(solution)/shard_map/fetch/ppermute | solution.py:439
  28.7 4.9 %collective-permute-start.2 = (bf16[6,80,128]{2,1,0:T(8,128)(2,1)}, bf16[6,80,128]{2,1,0:T(8,128)(2,1)S(1)}, u32[]{:S(2)}, u32[]{:S(2)}) collective-permute-start(bf16[6,80,128]{2,1,0:T(8,128)(2,1)} %get-tuple-element.15.own_pred_ref), channel_id=1, source_target_pairs={{0,1},{4,7},{8,9},{12,15},{16,17},{20,23},{24,25},{28,31},{32,33},... | collective-permute-start | bytes 368648 | tf_op jit(solution)/shard_map/fetch/ppermute | solution.py:439
  32.3 4.7 %collective-permute-start.3 = (bf16[3,80,128]{2,1,0:T(8,128)(2,1)S(1)}, bf16[3,80,128]{2,1,0:T(8,128)(2,1)S(1)}, u32[]{:S(2)}, u32[]{:S(2)}) collective-permute-start(bf16[3,80,128]{2,1,0:T(8,128)(2,1)S(1)} %constant_dynamic-slice_fusion), channel_id=1, source_target_pairs={{0,2},{4,6},{8,10},{12,14},{16,18},{20,22},{24,26},{28,30},{32,34}... | collective-permute-start | bytes 184328 | tf_op jit(solution)/shard_map/fetch/ppermute | solution.py:439
  37.0 1.7 %collective-permute-start.5 = (bf16[17,80,128]{2,1,0:T(8,128)(2,1)S(1)}, bf16[17,80,128]{2,1,0:T(8,128)(2,1)S(1)}, u32[]{:S(2)}, u32[]{:S(2)}) collective-permute-start(bf16[17,80,128]{2,1,0:T(8,128)(2,1)S(1)} %constant_dynamic-update-slice_fusion.mine_ref), channel_id=1, source_target_pairs={{0,4},{4,0},{8,12},{12,8},{16,20},{20,16},{24,28},{28,24},{32,36},... | collective-permute-start | bytes 1044488 | tf_op jit(solution)/shard_map/fetch/ppermute | solution.py:452
  37.2 2.0 %collective-permute-start.4 = (bf16[16,80,128]{2,1,0:T(8,128)(2,1)S(1)}, bf16[16,80,128]{2,1,0:T(8,128)(2,1)S(1)}, u32[]{:S(2)}, u32[]{:S(2)}) collective-permute-start(bf16[16,80,128]{2,1,0:T(8,128)(2,1)S(1)} %collective-permute-done.near_mine_ref), channel_id=1, source_target_pairs={{0,4},{4,0},{8,12},{12,8},{16,20},{20,16},{24,28},{28,24},{32,36},... | collective-permute-start | bytes 983048 | tf_op jit(solution)/shard_map/fetch/ppermute | solution.py:451
  58.2 6.7 %collective-permute-start.6 = (f32[3,24,320]{2,1,0:T(8,128)S(1)}, f32[3,24,320]{2,1,0:T(8,128)S(1)}, u32[]{:S(2)}, u32[]{:S(2)}) collective-permute-start(f32[3,24,320]{2,1,0:T(8,128)S(1)} %pad_maximum_fusion), channel_id=1, source_target_pairs={{0,2},{1,3},{2,0},{3,1},{4,6},{5,7},{6,4},{7,5},{8,10},{9,11},{10,... | collective-permute-start | bytes 276488 | tf_op jit(solution)/shard_map/combine_vocab/ppermute | solution.py:419
  62.2 5.2 %collective-permute-start.7 = (f32[3,24,320]{2,1,0:T(8,128)S(1)}, f32[3,24,320]{2,1,0:T(8,128)S(1)}, u32[]{:S(2)}, u32[]{:S(2)}) collective-permute-start(f32[3,24,320]{2,1,0:T(8,128)S(1)} %pad_maximum_fusion), channel_id=1, source_target_pairs={{0,1},{1,2},{2,3},{3,0},{4,5},{5,6},{6,7},{7,4},{8,9},{9,10},{10,1... | collective-permute-start | bytes 276488 | tf_op jit(solution)/shard_map/combine_vocab/ppermute | solution.py:419
  62.2 5.2 %collective-permute-start.8 = (f32[3,24,320]{2,1,0:T(8,128)S(1)}, f32[3,24,320]{2,1,0:T(8,128)S(1)}, u32[]{:S(2)}, u32[]{:S(2)}) collective-permute-start(f32[3,24,320]{2,1,0:T(8,128)S(1)} %pad_maximum_fusion), channel_id=1, source_target_pairs={{0,3},{1,0},{2,1},{3,2},{4,7},{5,4},{6,5},{7,6},{8,11},{9,8},{10,9... | collective-permute-start | bytes 276488 | tf_op jit(solution)/shard_map/combine_vocab/ppermute | solution.py:419

commit v5 on v4

--- a/solution.py
+++ b/solution.py
@@ -18,7 +18,7 @@
 BATCH_WAYS = 4
 
 
-def pack_kernel(weight_ref, pred_ref, labels_ref, block_ref, packed_ref):
+def pack_kernel(weight_ref, pred_ref, labels_ref, block_ref, packed_ref, half_ref):
     mine, odd_block = lax.axis_index("label"), lax.rem(lax.axis_index("tm"), 2) == 1
     tiles, positions, _ = packed_ref.shape
     rows = block_ref.shape[0]
@@ -40,6 +40,10 @@
     low = jnp.sum((own & 63).astype(F32), axis=1, keepdims=True)
     lane = lax.broadcasted_iota(jnp.int32, (positions, 128), 1)
     packed_ref[tiles - 1] = jnp.where(lane == 0, high, jnp.where(lane == 1, low, 0.0)).astype(BF16)
+    some = tiles // 2
+    for tile in range(some):
+        early, late = packed_ref[tile].astype(F32), packed_ref[some + tile].astype(F32)
+        half_ref[tile] = jnp.where(odd_block, late, early).astype(BF16)
 
 
 def pack(weight, pred, labels):
@@ -50,9 +54,10 @@
         out_shape=(
             jax.ShapeDtypeStruct((weight.shape[0] // 2, 128), BF16),
             jax.ShapeDtypeStruct((width // 128 + 1, positions, 128), BF16),
+            jax.ShapeDtypeStruct(((width // 128 + 1) // 2, positions, 128), BF16),
         ),
         in_specs=[vmem] * 3,
-        out_specs=(vmem, vmem),
+        out_specs=(vmem,) * 3,
         name="pack",
     )(weight, pred, labels)
 
@@ -422,7 +427,7 @@
     return [array] + moved
 
 
-def both_ways(array, axis):
+def both_ways(array, axis, half=None):
     ways, cores = lax.axis_size(axis), lax.axis_size("tm")
     axes = ("batch", "tm") if axis == "batch" else ("tm", "label")
 
@@ -434,19 +439,20 @@
         for at in range(cores):
             near.append((device(way, at), device(way + (1 if at % 2 == 0 else -1), at)))
             opposite.append((device(way, at), device(way + 2, at)))
-    some = array.shape[0] // 2
-    half = lax.dynamic_slice_in_dim(array, lax.axis_index("tm") % 2 * some, some, axis=0)
+    if half is None:
+        some = array.shape[0] // 2
+        half = lax.dynamic_slice_in_dim(array, lax.axis_index("tm") % 2 * some, some, axis=0)
     return lax.ppermute(array, axes, near), lax.ppermute(half, axes, opposite)
 
 
 def shards(enc_joint, pred_joint, out_weight, labels, frame_len, label_len):
     mine = lax.axis_index("label")
-    own, own_pred = pack(out_weight, pred_joint[0], labels)
+    own, own_pred, half_pred = pack(out_weight, pred_joint[0], labels)
     with jax.named_scope("gather_weight"):
         own = lax.all_gather(own, "tm", axis=0, tiled=False)
     with jax.named_scope("fetch"):
         near, opposite = both_ways(own, "batch")
-        rest = jnp.concatenate([opposite, *both_ways(own_pred, "label")], axis=0)
+        rest = jnp.concatenate([opposite, *both_ways(own_pred, "label", half_pred)], axis=0)
         swap = [(i, i ^ 1) for i in range(lax.axis_size("tm"))]
         near_theirs = lax.ppermute(near, "tm", swap)
         theirs = lax.ppermute(rest, "tm", swap)

time: 95.4 us -> 95.9 us (level)
  starting transfers between devices: 12.6 us -> 14 us
    ppermute x1, waiting for transfers between devices: 1.14 us -> 0.07 us  [shards(): theirs = lax.ppermute(rest, 'tm', swap)]
    ppermute x1, starting transfers between devices: 0.38 us -> 1.35 us  [shards(): near_theirs = lax.ppermute(near, 'tm', swap)]
  transfers between devices with their start and end apart: 9 -> 9, of which waited for: 5 -> 6; matrix products, arithmetic and copies ran while one was open for 1% -> 0% of each run, Pallas kernels for 0% -> 0%
where the time goes in v5:
time: 95.9 us; the launch traced here: 95.7 us
  blocking collectives  41.9 us (44%)
  Pallas kernels  28.9 us (30%)
  starting transfers between devices  14 us (15%)
  waiting for transfers between devices  8.36 us (9%)
  between operations  2.01 us (2%)
    all_gather x1, blocking collectives, shards(): own = lax.all_gather(own, 'tm', axis=0, tiled=False)  22.6 us
    all_gather x1, blocking collectives, shards(): lax.all_gather(jnp.stack([log_blank, log_label]), 'tm', axis=0, tiled=False)  19.4 us
    pallas_call x1, Pallas kernels, joint_terms(): pl.pallas_call(joint_kernel, out_shape=(grouped, grouped, jax.ShapeDtypeS...  18.8 us
    pallas_call x1, Pallas kernels, lattice_loss(): pl.pallas_call(lattice_kernel, out_shape=(jax.ShapeDtypeStruct((1, 1), F3...  8.36 us
    ppermute x4, starting transfers between devices, both_ways(): return (lax.ppermute(array, axes, near), lax.ppermute(half, axes, opposite))  6.77 us
    ppermute x3, starting transfers between devices, around(): lax.ppermute(array, axis, [(i, (i + by) % size) for i in range(size)])  5.58 us
    ppermute x4, waiting for transfers between devices, both_ways(): return (lax.ppermute(array, axes, near), lax.ppermute(half, axes, opposite))  4.68 us
    ppermute x3, waiting for transfers between devices, around(): lax.ppermute(array, axis, [(i, (i + by) % size) for i in range(size)])  2.43 us
  transfers between devices with their start and end apart: 9, of which 6 were waited for; matrix products, arithmetic and copies ran while one was open for 0% of the time, Pallas kernels for 0%

profile of v5, /device:TPU:1, one launch (start us, length us, event | category | flops | bytes accessed | tf_op | source)
XLA Modules:
  0.0 95.7 jit_solution(3084420575084316806)
XLA Ops:
  0.6 0.0 copy-start.1
  0.7 1.7 %pack.1 = (bf16[80,128]{1,0:T(8,128)(2,1)}, bf16[6,80,128]{2,1,0:T(8,128)(2,1)}, bf16[3,80,128]{2,1,0:T(8,128)(2,1)}) custom-call(bf16[160,256]{1,0:T(8,128)(2,1)} %weight_ref.1, bf16[80,640]{1,0:T(8,128)(2,1)} %bitcast.62, s32[1,80]{1,0:T(1,128)} %labels_ref.1), custom_call_target="tpu_custom_call" | custom-call | tf_op jit(solution)/shard_map/pack/pallas_call | solution.py:52
  2.4 0.0 copy-start
  2.4 22.6 %all-gather = bf16[1280,128]{1,0:T(8,128)(2,1)S(1)} all-gather(bf16[80,128]{1,0:T(8,128)(2,1)} %get-tuple-element.15), channel_id=2, replica_groups=mesh['batch'=4,'tm'=16,'label'=4] {'tm'}, dimensions={0}, use_global_device_ids=true | all-gather | bytes 348160 | tf_op jit(solution)/shard_map/gather_weight/all_gather | solution.py:452
  25.0 2.8 %collective-permute-start.1 = (bf16[8,80,128]{2,1,0:T(8,128)(2,1)S(1)}, bf16[8,80,128]{2,1,0:T(8,128)(2,1)S(1)}, u32[]{:S(2)}, u32[]{:S(2)}) collective-permute-start(bf16[8,80,128]{2,1,0:T(8,128)(2,1)S(1)} %constant_dynamic-slice_fusion), channel_id=1, source_target_pairs={{0,128},{4,132},{8,136},{12,140},{16,144},{20,148},{24,152},{28,15... | collective-permute-start | bytes 491528 | tf_op jit(solution)/shard_map/fetch/ppermute | solution.py:445
  27.8 2.7 %collective-permute-start.2 = (bf16[6,80,128]{2,1,0:T(8,128)(2,1)}, bf16[6,80,128]{2,1,0:T(8,128)(2,1)S(1)}, u32[]{:S(2)}, u32[]{:S(2)}) collective-permute-start(bf16[6,80,128]{2,1,0:T(8,128)(2,1)} %get-tuple-element.16.own_pred_ref), channel_id=1, source_target_pairs={{0,1},{4,7},{8,9},{12,15},{16,17},{20,23},{24,25},{28,31},{32,33},... | collective-permute-start | bytes 368648 | tf_op jit(solution)/shard_map/fetch/ppermute | solution.py:445
  30.5 0.9 collective-permute-start
  31.4 0.3 collective-permute-start.3
  31.8 0.5 collective-permute-done.1
  32.2 0.5 collective-permute-done.2
  32.8 3.7 %collective-permute-done.3 = bf16[3,80,128]{2,1,0:T(8,128)(2,1)S(1)} collective-permute-done((bf16[3,80,128]{2,1,0:T(8,128)(2,1)}, bf16[3,80,128]{2,1,0:T(8,128)(2,1)S(1)}, u32[]{:S(2)}, u32[]{:S(2)}) %collective-permute-start.3) | collective-permute-done | bytes 61472 | tf_op jit(solution)/shard_map/fetch/ppermute | solution.py:445
  36.4 0.3 collective-permute-start.5
  36.7 0.0 collective-permute-done.near_mine_ref
  36.8 1.4 %collective-permute-start.4 = (bf16[16,80,128]{2,1,0:T(8,128)(2,1)S(1)}, bf16[16,80,128]{2,1,0:T(8,128)(2,1)S(1)}, u32[]{:S(2)}, u32[]{:S(2)}) collective-permute-start(bf16[16,80,128]{2,1,0:T(8,128)(2,1)S(1)} %collective-permute-done.near_mine_ref), channel_id=1, source_target_pairs={{0,4},{4,0},{8,12},{12,8},{16,20},{20,16},{24,28},{28,24},{32,36},... | collective-permute-start | bytes 983048 | tf_op jit(solution)/shard_map/fetch/ppermute | solution.py:457
  38.1 0.1 collective-permute-done.5.theirs_ref
  38.2 1.2 %collective-permute-done.4.near_theirs_ref = bf16[16,80,128]{2,1,0:T(8,128)(2,1)S(1)} collective-permute-done((bf16[16,80,128]{2,1,0:T(8,128)(2,1)S(1)}, bf16[16,80,128]{2,1,0:T(8,128)(2,1)S(1)}, u32[]{:S(2)}, u32[]{:S(2)}) %collective-permute-start.4) | collective-permute-done | bytes 327712 | tf_op jit(solution)/shard_map/fetch/ppermute | solution.py:457
  39.4 0.0 copy-done.1
  39.4 0.0 copy-done
  39.4 18.8 %joint.1 = (f32[6,1280]{1,0:T(8,128)S(1)}, f32[6,1280]{1,0:T(8,128)S(1)}, f32[24,320]{1,0:T(8,128)S(1)}) custom-call(bf16[24,640]{1,0:T(8,128)(2,1)S(1)} %bitcast.61, bf16[16,80,128]{2,1,0:T(8,128)(2,1)S(1)} %bitcast.59, bf16[6,80,128]{2,1,0:T(8,128)(2,1)S(1)} %copy-done, bf16[16,80,128]{2,1,0:T(8,128)(2,1)S(1)} %collective-permute-done.near_mine_ref, ...), custom_call_target="tpu_custom_call" | custom-call | flops 10066329600 | bytes 2097152 | tf_op jit(solution)/shard_map/joint/pallas_call | solution.py:198
  58.2 0.1 reshape.32
  58.3 0.1 reshape.31
  58.4 2.9 %collective-permute-start.6 = (f32[3,24,320]{2,1,0:T(8,128)S(1)}, f32[3,24,320]{2,1,0:T(8,128)S(1)}, u32[]{:S(2)}, u32[]{:S(2)}) collective-permute-start(f32[3,24,320]{2,1,0:T(8,128)S(1)} %pad_maximum_fusion), channel_id=1, source_target_pairs={{0,2},{1,3},{2,0},{3,1},{4,6},{5,7},{6,4},{7,5},{8,10},{9,11},{10,... | collective-permute-start | bytes 276488 | tf_op jit(solution)/shard_map/combine_vocab/ppermute | solution.py:424
  62.6 0.1 reshape.33
  62.6 0.1 reshape.30
  62.7 0.0 collective-permute-start.7
  62.8 2.7 %collective-permute-start.8 = (f32[3,24,320]{2,1,0:T(8,128)S(1)}, f32[3,24,320]{2,1,0:T(8,128)S(1)}, u32[]{:S(2)}, u32[]{:S(2)}) collective-permute-start(f32[3,24,320]{2,1,0:T(8,128)S(1)} %pad_maximum_fusion), channel_id=1, source_target_pairs={{0,3},{1,0},{2,1},{3,2},{4,7},{5,4},{6,5},{7,6},{8,11},{9,8},{10,9... | collective-permute-start | bytes 276488 | tf_op jit(solution)/shard_map/combine_vocab/ppermute | solution.py:424
  65.4 0.0 collective-permute-done.6
  65.5 2.4 %collective-permute-done.7 = f32[3,24,320]{2,1,0:T(8,128)S(1)} collective-permute-done((f32[3,24,320]{2,1,0:T(8,128)S(1)}, f32[3,24,320]{2,1,0:T(8,128)S(1)}, u32[]{:S(2)}, u32[]{:S(2)}) %collective-permute-start.7) | collective-permute-done | bytes 92192 | tf_op jit(solution)/shard_map/combine_vocab/ppermute | solution.py:424
  67.9 0.0 collective-permute-done.8
  67.9 0.1 fusion.7
  68.0 19.4 %all-gather.1 = f32[32,24,320]{2,1,0:T(8,128)S(1)} all-gather(f32[2,24,320]{2,1,0:T(8,128)S(1)} %pad_maximum_fusion.1), channel_id=3, replica_groups=mesh['batch'=4,'tm'=16,'label'=4] {'tm'}, dimensions={0}, use_global_device_ids=true | all-gather | bytes 1044480 | tf_op jit(solution)/shard_map/gather_grid/all_gather | solution.py:472
  87.3 8.4 %lattice.1 = (f32[1,1]{1,0:T(1,128)}, f32[24,80]{1,0:T(8,128)}, f32[24,80]{1,0:T(8,128)}) custom-call(s32[1]{0:T(128)S(6)} %copy.11.frame_len_ref, s32[1]{0:T(128)S(6)} %copy.12.label_len_ref, f32[16,2,24,320]{3,2,1,0:T(8,128)S(1)} %bitcast.56), custom_call_target="tpu_custom_call" | custom-call | tf_op jit(solution)/shard_map/lattice/pallas_call | solution.py:403
  (8 shorter events, 0.1 us)
Async XLA Ops:
  0.6 38.7 %copy-start.1 = (bf16[1,24,640]{2,1,0:T(8,128)(2,1)S(1)}, bf16[1,24,640]{2,1,0:T(8,128)(2,1)}, u32[]{:S(2)}) copy-start(bf16[1,24,640]{2,1,0:T(8,128)(2,1)} %param.6) | copy-start | bytes 92164
  2.4 37.0 %copy-start = (bf16[6,80,128]{2,1,0:T(8,128)(2,1)S(1)}, bf16[6,80,128]{2,1,0:T(8,128)(2,1)}, u32[]{:S(2)}) copy-start(bf16[6,80,128]{2,1,0:T(8,128)(2,1)} %get-tuple-element.16.own_pred_ref) | copy-start | bytes 368644
  25.0 7.2 %collective-permute-start.1 = (bf16[8,80,128]{2,1,0:T(8,128)(2,1)S(1)}, bf16[8,80,128]{2,1,0:T(8,128)(2,1)S(1)}, u32[]{:S(2)}, u32[]{:S(2)}) collective-permute-start(bf16[8,80,128]{2,1,0:T(8,128)(2,1)S(1)} %constant_dynamic-slice_fusion), channel_id=1, source_target_pairs={{0,128},{4,132},{8,136},{12,140},{16,144},{20,148},{24,152},{28,15... | collective-permute-start | bytes 491528 | tf_op jit(solution)/shard_map/fetch/ppermute | solution.py:445
  27.8 4.9 %collective-permute-start.2 = (bf16[6,80,128]{2,1,0:T(8,128)(2,1)}, bf16[6,80,128]{2,1,0:T(8,128)(2,1)S(1)}, u32[]{:S(2)}, u32[]{:S(2)}) collective-permute-start(bf16[6,80,128]{2,1,0:T(8,128)(2,1)} %get-tuple-element.16.own_pred_ref), channel_id=1, source_target_pairs={{0,1},{4,7},{8,9},{12,15},{16,17},{20,23},{24,25},{28,31},{32,33},... | collective-permute-start | bytes 368648 | tf_op jit(solution)/shard_map/fetch/ppermute | solution.py:445
  30.5 6.2 %collective-permute-start = (bf16[16,80,128]{2,1,0:T(8,128)(2,1)S(1)}, bf16[16,80,128]{2,1,0:T(8,128)(2,1)S(1)}, u32[]{:S(2)}, u32[]{:S(2)}) collective-permute-start(bf16[16,80,128]{2,1,0:T(8,128)(2,1)S(1)} %bitcast.58), channel_id=1, source_target_pairs={{0,64},{4,196},{8,72},{12,204},{16,80},{20,212},{24,88},{28,220},{... | collective-permute-start | bytes 983048 | tf_op jit(solution)/shard_map/fetch/ppermute | solution.py:445
  31.4 5.0 %collective-permute-start.3 = (bf16[3,80,128]{2,1,0:T(8,128)(2,1)}, bf16[3,80,128]{2,1,0:T(8,128)(2,1)S(1)}, u32[]{:S(2)}, u32[]{:S(2)}) collective-permute-start(bf16[3,80,128]{2,1,0:T(8,128)(2,1)} %get-tuple-element.17), channel_id=1, source_target_pairs={{0,2},{4,6},{8,10},{12,14},{16,18},{20,22},{24,26},{28,30},{32,34}... | collective-permute-start | bytes 184328 | tf_op jit(solution)/shard_map/fetch/ppermute | solution.py:445
  36.4 1.7 %collective-permute-start.5 = (bf16[17,80,128]{2,1,0:T(8,128)(2,1)S(1)}, bf16[17,80,128]{2,1,0:T(8,128)(2,1)S(1)}, u32[]{:S(2)}, u32[]{:S(2)}) collective-permute-start(bf16[17,80,128]{2,1,0:T(8,128)(2,1)S(1)} %constant_dynamic-update-slice_fusion.mine_ref), channel_id=1, source_target_pairs={{0,4},{4,0},{8,12},{12,8},{16,20},{20,16},{24,28},{28,24},{32,36},... | collective-permute-start | bytes 1044488 | tf_op jit(solution)/shard_map/fetch/ppermute | solution.py:458
  36.8 2.6 %collective-permute-start.4 = (bf16[16,80,128]{2,1,0:T(8,128)(2,1)S(1)}, bf16[16,80,128]{2,1,0:T(8,128)(2,1)S(1)}, u32[]{:S(2)}, u32[]{:S(2)}) collective-permute-start(bf16[16,80,128]{2,1,0:T(8,128)(2,1)S(1)} %collective-permute-done.near_mine_ref), channel_id=1, source_target_pairs={{0,4},{4,0},{8,12},{12,8},{16,20},{20,16},{24,28},{28,24},{32,36},... | collective-permute-start | bytes 983048 | tf_op jit(solution)/shard_map/fetch/ppermute | solution.py:457
  58.4 7.1 %collective-permute-start.6 = (f32[3,24,320]{2,1,0:T(8,128)S(1)}, f32[3,24,320]{2,1,0:T(8,128)S(1)}, u32[]{:S(2)}, u32[]{:S(2)}) collective-permute-start(f32[3,24,320]{2,1,0:T(8,128)S(1)} %pad_maximum_fusion), channel_id=1, source_target_pairs={{0,2},{1,3},{2,0},{3,1},{4,6},{5,7},{6,4},{7,5},{8,10},{9,11},{10,... | collective-permute-start | bytes 276488 | tf_op jit(solution)/shard_map/combine_vocab/ppermute | solution.py:424
  62.7 5.2 %collective-permute-start.7 = (f32[3,24,320]{2,1,0:T(8,128)S(1)}, f32[3,24,320]{2,1,0:T(8,128)S(1)}, u32[]{:S(2)}, u32[]{:S(2)}) collective-permute-start(f32[3,24,320]{2,1,0:T(8,128)S(1)} %pad_maximum_fusion), channel_id=1, source_target_pairs={{0,1},{1,2},{2,3},{3,0},{4,5},{5,6},{6,7},{7,4},{8,9},{9,10},{10,1... | collective-permute-start | bytes 276488 | tf_op jit(solution)/shard_map/combine_vocab/ppermute | solution.py:424
  62.8 5.1 %collective-permute-start.8 = (f32[3,24,320]{2,1,0:T(8,128)S(1)}, f32[3,24,320]{2,1,0:T(8,128)S(1)}, u32[]{:S(2)}, u32[]{:S(2)}) collective-permute-start(f32[3,24,320]{2,1,0:T(8,128)S(1)} %pad_maximum_fusion), channel_id=1, source_target_pairs={{0,3},{1,0},{2,1},{3,2},{4,7},{5,4},{6,5},{7,6},{8,11},{9,8},{10,9... | collective-permute-start | bytes 276488 | tf_op jit(solution)/shard_map/combine_vocab/ppermute | solution.py:424
